TPU v7x, 32 devices: a whole 2x2x4 slice. The times are simulated.
32 devices in a mesh: parts: 2 (over y), block: 4 (over z), shot: 2 (over x), sub: 2 (over core).
Axes of the slice: x: 2, y: 2, z: 4, core: 2. Of those that a mesh axis runs over, the one named last changes fastest.
Arguments:
- vel_sq: float32 [8, 16, 16, 128], P(('parts', 'block'), None, 'sub'), parts along dimension 0, may hold values from 0.06 to 0.18
- fwd_state: bfloat16 [16, 2, 80, 16, 128], P(('parts', 'block', 'shot'), None, None, 'sub'), parts along dimension 0, may hold values from -6 to 6
- adj_state: bfloat16 [16, 2, 80, 16, 128], P(('parts', 'block', 'shot'), None, None, 'sub'), parts along dimension 0, may hold values from -6 to 6
- wavelet: float32 [16, 4], P(('parts', 'block', 'shot')), parts along dimension 0, may hold values from -12 to 12
- source: int32 [16, 3], P(('parts', 'block', 'shot')), parts along dimension 0, may hold values from 0 to 127, as said below
- aperture: int32 [16, 2], P(('parts', 'block', 'shot')), parts along dimension 0, may hold values from 0 to 2
- rec_mask: int32 [16, 80, 16], P(('parts', 'block', 'shot'), None, 'sub'), parts along dimension 0, may hold values 0 or 1
- rec_data: float32 [16, 4, 80, 16], P(('parts', 'block', 'shot'), None, None, 'sub'), parts along dimension 0, may hold values from -6 to 6
Outputs:
- image: float32 [8, 16, 16, 128], P(('parts', 'block'), None, 'sub', 'shot'), parts along dimension 0
There are 2 independent parts, one for each index of `parts`. A program takes and returns all parts, laid end to end along the dimension named above; each array names one. Nothing has to cross between parts.
Inputs may be any that keep to these rules, and one draw needn't show every extreme that they name: source offsets lie in the home block, second coordinate below 16, depth below 128.
All inputs are finite; a program needn't handle non-finite values. No bound on the sum of `rec_mask` on one device may be relied on, other than what follows from the above.
Results may differ from a plain program's by a relative error of at most 0.0003.
Values may be sent and summed in bfloat16 or wider, within the bound.
A program may use at most 64 MiB of HBM per device.

v0:
```python
import jax
import jax.numpy as jnp
from jax import lax
from jax.sharding import PartitionSpec as P

R = 2
STEPS = 4


coeffs = (-205.0 / 72.0, 8.0 / 5.0, -1.0 / 5.0, 8.0 / 315.0, -1.0 / 560.0)
image_scale = 0.05


def with_halo(block, sides, width):
    for axis, dim in sides:
        count = lax.axis_size(axis)
        forward = [(i, i + 1) for i in range(count - 1)]
        backward = [(target, source) for source, target in forward]
        low = lax.ppermute(
            lax.slice_in_dim(block, block.shape[dim] - width, None, axis=dim), axis, forward
        )
        high = lax.ppermute(lax.slice_in_dim(block, 0, width, axis=dim), axis, backward)
        block = jnp.concatenate([low, block, high], axis=dim)
    return block


def passed_along(value, axis, by):
    peers = lax.axis_size(axis)
    pairs = [(i, i + by) for i in range(peers) if 0 <= i + by < peers]
    return lax.ppermute(value, axis, pairs)


def stencil(field, wide):
    sx, sy, sz = field.shape
    padded = jnp.pad(wide, ((4, 4), (0, 0), (4, 4)))
    total = 3.0 * coeffs[0] * field
    for step in range(1, 5):
        total = total + coeffs[step] * (
            padded[4 + step : 4 + step + sx, 4 : 4 + sy, 4 : 4 + sz]
            + padded[4 - step : 4 - step + sx, 4 : 4 + sy, 4 : 4 + sz]
        )
        total = total + coeffs[step] * (
            padded[4 : 4 + sx, 4 + step : 4 + step + sy, 4 : 4 + sz]
            + padded[4 : 4 + sx, 4 - step : 4 - step + sy, 4 : 4 + sz]
        )
        total = total + coeffs[step] * (
            padded[4 : 4 + sx, 4 : 4 + sy, 4 + step : 4 + step + sz]
            + padded[4 : 4 + sx, 4 : 4 + sy, 4 - step : 4 - step + sz]
        )
    return total


def laplace_rims(field):
    wide = with_halo(field, (("sub", 1),), 4)
    return stencil(field, wide)


def shards(vel_sq, fwd_state, adj_state, wavelet, source, aperture, rec_mask, rec_data):
    blocks = 2 * R + 1
    own_block = vel_sq[0]
    bx, bys, bz = own_block.shape
    width = blocks * bx
    nblock = lax.axis_size("block")
    home = lax.axis_index("block")
    ylow = lax.axis_index("sub") * bys
    pieces = []
    for offset in range(blocks):
        if offset == R:
            pieces.append(own_block)
        else:
            pieces.append(passed_along(own_block, "block", R - offset))
    window = jnp.concatenate(pieces, 0)
    injects = rec_mask[0].astype(jnp.float32)[None] * rec_data[0]
    states = jnp.concatenate([fwd_state[0], adj_state[0]], 0)
    ycells = window.shape[1]
    ap = aperture[0]
    src = source[0]
    index = jnp.arange(blocks, dtype=jnp.int32)
    inside = (
        (index >= R - ap[0])
        & (index <= R + ap[1])
        & (home - R + index >= 0)
        & (home - R + index < nblock)
    )
    keep = jnp.repeat(inside.astype(jnp.float32), bx)[:, None, None]
    xpos = lax.broadcasted_iota(jnp.int32, (width, ycells, bz), 0)
    ypos = lax.broadcasted_iota(jnp.int32, (width, ycells, bz), 1) + ylow
    zpos = lax.broadcasted_iota(jnp.int32, (width, ycells, bz), 2)
    onehot = ((xpos == R * bx + src[0]) & (ypos == src[1]) & (zpos == src[2])).astype(jnp.float32)
    surface = (jnp.arange(bz) == 0).astype(jnp.float32)[None, None, :]
    wav = wavelet[0]
    f_prev = keep * states[0].astype(jnp.float32)
    f_now = keep * states[1].astype(jnp.float32)
    stored = [f_now]
    for step in range(STEPS):
        f_next = keep * (2.0 * f_now - f_prev + window * laplace_rims(f_now) + wav[step] * onehot)
        f_prev, f_now = (f_now, f_next)
        stored.append(f_now)
    a_next = keep * states[2].astype(jnp.float32)
    a_now = keep * states[3].astype(jnp.float32)
    partial_value = stored[STEPS] * a_now
    for step in range(STEPS):
        later = STEPS - 1 - step
        inject = injects[later][:, :, None] * surface
        a_prev = keep * (2.0 * a_now - a_next + window * laplace_rims(a_now) + inject)
        a_next, a_now = (a_now, a_prev)
        partial_value = partial_value + stored[later] * a_now
    partial_value = partial_value.reshape(blocks, bx, bys, bz)
    gathered = partial_value[R]
    for offset in range(blocks):
        if offset != R:
            gathered = gathered + passed_along(partial_value[offset], "block", offset - R)
    total = lax.psum_scatter(gathered, "shot", scatter_dimension=2, tiled=True)
    return (image_scale * total)[None]


def solution(mesh):
    placed = (
        P(("parts", "block"), None, "sub", None),
        P(("parts", "block", "shot"), None, None, "sub", None),
        P(("parts", "block", "shot"), None, None, "sub", None),
        P(("parts", "block", "shot"), None),
        P(("parts", "block", "shot"), None),
        P(("parts", "block", "shot"), None),
        P(("parts", "block", "shot"), None, "sub"),
        P(("parts", "block", "shot"), None, None, "sub"),
    )
    return jax.shard_map(
        shards,
        mesh=mesh,
        in_specs=placed,
        out_specs=P(("parts", "block"), None, "sub", "shot"),
        check_vma=False,
    )
```

profile of v0, /device:TPU:0, one launch (start us, length us, event | category | flops | bytes accessed | tf_op | source)
XLA Modules:
  0.0 126.6 jit_solution(4158335523889276605)
XLA Ops:
  6.6 1.4 %collective-permute-start.3 = (f32[16,8,128]{2,1,0:T(8,128)}, f32[16,8,128]{2,1,0:T(8,128)S(1)}, u32[]{:S(2)}, u32[]{:S(2)}) collective-permute-start(f32[16,8,128]{2,1,0:T(8,128)} %bitcast.49), channel_id=1, source_target_pairs={{8,0},{12,4},{9,1},{13,5},{10,2},{14,6},{11,3},{15,7},{24,16},{28,... | collective-permute-start | bytes 196616 | tf_op jit(solution)/shard_map/ppermute | solution.py:30
  8.0 1.3 %collective-permute-start.2 = (f32[16,8,128]{2,1,0:T(8,128)}, f32[16,8,128]{2,1,0:T(8,128)S(1)}, u32[]{:S(2)}, u32[]{:S(2)}) collective-permute-start(f32[16,8,128]{2,1,0:T(8,128)} %bitcast.50), channel_id=1, source_target_pairs={{4,0},{8,4},{12,8},{5,1},{9,5},{13,9},{6,2},{10,6},{14,10},{7,3},{... | collective-permute-start | bytes 196616 | tf_op jit(solution)/shard_map/ppermute | solution.py:30
  9.3 5.6 %collective-permute-start.1 = (f32[16,8,128]{2,1,0:T(8,128)}, f32[16,8,128]{2,1,0:T(8,128)S(1)}, u32[]{:S(2)}, u32[]{:S(2)}) collective-permute-start(f32[16,8,128]{2,1,0:T(8,128)} %bitcast.51), channel_id=1, source_target_pairs={{0,4},{4,8},{8,12},{1,5},{5,9},{9,13},{2,6},{6,10},{10,14},{3,7},{... | collective-permute-start | bytes 196616 | tf_op jit(solution)/shard_map/ppermute | solution.py:30
  14.9 4.9 %collective-permute-start = (f32[16,8,128]{2,1,0:T(8,128)}, f32[16,8,128]{2,1,0:T(8,128)S(1)}, u32[]{:S(2)}, u32[]{:S(2)}) collective-permute-start(f32[16,8,128]{2,1,0:T(8,128)} %bitcast.52), channel_id=1, source_target_pairs={{0,8},{4,12},{1,9},{5,13},{2,10},{6,14},{3,11},{7,15},{16,24},{20,... | collective-permute-start | bytes 196616 | tf_op jit(solution)/shard_map/ppermute | solution.py:30
  19.8 1.3 %fusion.329 = (s32[1,1]{1,0:T(1,128)}, s32[1,1]{1,0:T(1,128)}) fusion(s32[1,2]{1,0:T(1,128)} %param.13), kind=kLoop, calls=%fused_computation.548 | loop fusion | bytes 16 | tf_op jit(solution)/shard_map/slice | solution.py:80
  23.9 1.3 %collective-permute-start.5 = (f32[80,4,128]{2,1,0:T(4,128)S(1)}, f32[80,4,128]{2,1,0:T(4,128)S(1)}, u32[]{:S(2)}, u32[]{:S(2)}) collective-permute-start(f32[80,4,128]{2,1,0:T(4,128)S(1)} %get-tuple-element.17), channel_id=1, source_target_pairs={{1,0},{3,2},{5,4},{7,6},{9,8},{11,10},{13,12},{15,14},{17,16},{19,... | collective-permute-start | bytes 491528 | tf_op jit(solution)/shard_map/ppermute | solution.py:22
  28.9 3.0 %collective-permute-start.4 = (f32[80,4,128]{2,1,0:T(4,128)S(1)}, f32[80,4,128]{2,1,0:T(4,128)S(1)}, u32[]{:S(2)}, u32[]{:S(2)}) collective-permute-start(f32[80,4,128]{2,1,0:T(4,128)S(1)} %get-tuple-element.18), channel_id=1, source_target_pairs={{0,1},{2,3},{4,5},{6,7},{8,9},{10,11},{12,13},{14,15},{16,17},{18,... | collective-permute-start | bytes 491528 | tf_op jit(solution)/shard_map/ppermute | solution.py:19
  32.0 1.3 %collective-permute-start.13 = (f32[80,4,128]{2,1,0:T(4,128)S(1)}, f32[80,4,128]{2,1,0:T(4,128)S(1)}, u32[]{:S(2)}, u32[]{:S(2)}) collective-permute-start(f32[80,4,128]{2,1,0:T(4,128)S(1)} %get-tuple-element.23), channel_id=1, source_target_pairs={{1,0},{3,2},{5,4},{7,6},{9,8},{11,10},{13,12},{15,14},{17,16},{19,... | collective-permute-start | bytes 491528 | tf_op jit(solution)/shard_map/ppermute | solution.py:22
  33.4 3.0 %collective-permute-start.12 = (f32[80,4,128]{2,1,0:T(4,128)S(1)}, f32[80,4,128]{2,1,0:T(4,128)S(1)}, u32[]{:S(2)}, u32[]{:S(2)}) collective-permute-start(f32[80,4,128]{2,1,0:T(4,128)S(1)} %get-tuple-element.24), channel_id=1, source_target_pairs={{0,1},{2,3},{4,5},{6,7},{8,9},{10,11},{12,13},{14,15},{16,17},{18,... | collective-permute-start | bytes 491528 | tf_op jit(solution)/shard_map/ppermute | solution.py:19
  38.2 1.7 %fusion.97 = f32[80,8,128]{2,1,0:T(8,128)S(1)} fusion(f32[80,8,128]{2,1,0:T(8,128)S(1)} %constant_dynamic-update-slice_fusion, f32[80,8,128]{2,1,0:T(8,128)S(1)} %get-tuple-element.37, f32[80,4,128]{2,1,0:T(4,128)S(1)} %collective-permute-done.12, f32[80,4,128]{2,1,0:T(4,128)S(1)} %collective-permute-done.13, f32[88,16,136]{2,1,0:T(8,128)S(1)} %select_maximum_fusion.6, ...), kind=kLoop, calls=%fused_computation.213 | loop fusion | flops 4423680 | bytes 6720832 | tf_op jit(solution)/shard_map/mul | solution.py:105
  40.0 1.4 %collective-permute-start.15 = (f32[80,4,128]{2,1,0:T(4,128)S(1)}, f32[80,4,128]{2,1,0:T(4,128)S(1)}, u32[]{:S(2)}, u32[]{:S(2)}) collective-permute-start(f32[80,4,128]{2,1,0:T(4,128)S(1)} %get-tuple-element.21), channel_id=1, source_target_pairs={{1,0},{3,2},{5,4},{7,6},{9,8},{11,10},{13,12},{15,14},{17,16},{19,... | collective-permute-start | bytes 491528 | tf_op jit(solution)/shard_map/ppermute | solution.py:22
  41.4 3.0 %collective-permute-start.14 = (f32[80,4,128]{2,1,0:T(4,128)S(1)}, f32[80,4,128]{2,1,0:T(4,128)S(1)}, u32[]{:S(2)}, u32[]{:S(2)}) collective-permute-start(f32[80,4,128]{2,1,0:T(4,128)S(1)} %get-tuple-element.22), channel_id=1, source_target_pairs={{0,1},{2,3},{4,5},{6,7},{8,9},{10,11},{12,13},{14,15},{16,17},{18,... | collective-permute-start | bytes 491528 | tf_op jit(solution)/shard_map/ppermute | solution.py:19
  45.2 2.4 %fusion.209 = f32[80,8,128]{2,1,0:T(8,128)S(1)} fusion(f32[80,8,128]{2,1,0:T(8,128)S(1)} %constant_dynamic-update-slice_fusion, f32[80,8,128]{2,1,0:T(8,128)S(1)} %get-tuple-element.36, f32[80,4,128]{2,1,0:T(4,128)S(1)} %collective-permute-done.4, f32[80,4,128]{2,1,0:T(4,128)S(1)} %collective-permute-done.5, f32[88,16,136]{2,1,0:T(8,128)S(1)} %select_maximum_fusion.14, ...), kind=kLoop, calls=%fused_computation.325 | loop fusion | flops 4587520 | bytes 6717980 | tf_op jit(solution)/shard_map/mul | solution.py:96
  47.7 1.3 %collective-permute-start.7 = (f32[80,4,128]{2,1,0:T(4,128)S(1)}, f32[80,4,128]{2,1,0:T(4,128)S(1)}, u32[]{:S(2)}, u32[]{:S(2)}) collective-permute-start(f32[80,4,128]{2,1,0:T(4,128)S(1)} %get-tuple-element.15), channel_id=1, source_target_pairs={{1,0},{3,2},{5,4},{7,6},{9,8},{11,10},{13,12},{15,14},{17,16},{19,... | collective-permute-start | bytes 491528 | tf_op jit(solution)/shard_map/ppermute | solution.py:22
  49.0 3.0 %collective-permute-start.6 = (f32[80,4,128]{2,1,0:T(4,128)S(1)}, f32[80,4,128]{2,1,0:T(4,128)S(1)}, u32[]{:S(2)}, u32[]{:S(2)}) collective-permute-start(f32[80,4,128]{2,1,0:T(4,128)S(1)} %get-tuple-element.16), channel_id=1, source_target_pairs={{0,1},{2,3},{4,5},{6,7},{8,9},{10,11},{12,13},{14,15},{16,17},{18,... | collective-permute-start | bytes 491528 | tf_op jit(solution)/shard_map/ppermute | solution.py:19
  52.8 1.7 %fusion.70 = f32[80,8,128]{2,1,0:T(8,128)S(1)} fusion(f32[80,8,128]{2,1,0:T(8,128)S(1)} %constant_dynamic-update-slice_fusion, f32[80,8,128]{2,1,0:T(8,128)S(1)} %fusion.97, f32[80,4,128]{2,1,0:T(4,128)S(1)} %collective-permute-done.14, f32[80,4,128]{2,1,0:T(4,128)S(1)} %collective-permute-done.15, f32[88,16,136]{2,1,0:T(8,128)S(1)} %select_maximum_fusion.4, ...), kind=kLoop, calls=%fused_computation.186 | loop fusion | flops 4423680 | bytes 6720832 | tf_op jit(solution)/shard_map/mul | solution.py:105
  54.6 1.3 %collective-permute-start.17 = (f32[80,4,128]{2,1,0:T(4,128)S(1)}, f32[80,4,128]{2,1,0:T(4,128)S(1)}, u32[]{:S(2)}, u32[]{:S(2)}) collective-permute-start(f32[80,4,128]{2,1,0:T(4,128)S(1)} %get-tuple-element.19), channel_id=1, source_target_pairs={{1,0},{3,2},{5,4},{7,6},{9,8},{11,10},{13,12},{15,14},{17,16},{19,... | collective-permute-start | bytes 491528 | tf_op jit(solution)/shard_map/ppermute | solution.py:22
  55.9 3.0 %collective-permute-start.16 = (f32[80,4,128]{2,1,0:T(4,128)S(1)}, f32[80,4,128]{2,1,0:T(4,128)S(1)}, u32[]{:S(2)}, u32[]{:S(2)}) collective-permute-start(f32[80,4,128]{2,1,0:T(4,128)S(1)} %get-tuple-element.20), channel_id=1, source_target_pairs={{0,1},{2,3},{4,5},{6,7},{8,9},{10,11},{12,13},{14,15},{16,17},{18,... | collective-permute-start | bytes 491528 | tf_op jit(solution)/shard_map/ppermute | solution.py:19
  59.7 2.4 %fusion.182 = f32[80,8,128]{2,1,0:T(8,128)S(1)} fusion(f32[80,8,128]{2,1,0:T(8,128)S(1)} %constant_dynamic-update-slice_fusion, f32[80,8,128]{2,1,0:T(8,128)S(1)} %fusion.209, f32[80,4,128]{2,1,0:T(4,128)S(1)} %collective-permute-done.6, f32[80,4,128]{2,1,0:T(4,128)S(1)} %collective-permute-done.7, f32[88,16,136]{2,1,0:T(8,128)S(1)} %select_maximum_fusion.12, ...), kind=kLoop, calls=%fused_computation.298 | loop fusion | flops 4587520 | bytes 6717980 | tf_op jit(solution)/shard_map/mul | solution.py:96
  62.2 1.3 %collective-permute-start.9 = (f32[80,4,128]{2,1,0:T(4,128)S(1)}, f32[80,4,128]{2,1,0:T(4,128)S(1)}, u32[]{:S(2)}, u32[]{:S(2)}) collective-permute-start(f32[80,4,128]{2,1,0:T(4,128)S(1)} %get-tuple-element.13), channel_id=1, source_target_pairs={{1,0},{3,2},{5,4},{7,6},{9,8},{11,10},{13,12},{15,14},{17,16},{19,... | collective-permute-start | bytes 491528 | tf_op jit(solution)/shard_map/ppermute | solution.py:22
  63.5 3.0 %collective-permute-start.8 = (f32[80,4,128]{2,1,0:T(4,128)S(1)}, f32[80,4,128]{2,1,0:T(4,128)S(1)}, u32[]{:S(2)}, u32[]{:S(2)}) collective-permute-start(f32[80,4,128]{2,1,0:T(4,128)S(1)} %get-tuple-element.14), channel_id=1, source_target_pairs={{0,1},{2,3},{4,5},{6,7},{8,9},{10,11},{12,13},{14,15},{16,17},{18,... | collective-permute-start | bytes 491528 | tf_op jit(solution)/shard_map/ppermute | solution.py:19
  67.3 1.7 %fusion.43 = f32[80,8,128]{2,1,0:T(8,128)S(1)} fusion(f32[80,8,128]{2,1,0:T(8,128)S(1)} %constant_dynamic-update-slice_fusion, f32[80,8,128]{2,1,0:T(8,128)S(1)} %fusion.70, f32[80,4,128]{2,1,0:T(4,128)S(1)} %collective-permute-done.16, f32[80,4,128]{2,1,0:T(4,128)S(1)} %collective-permute-done.17, f32[88,16,136]{2,1,0:T(8,128)S(1)} %select_maximum_fusion.2, ...), kind=kLoop, calls=%fused_computation.159 | loop fusion | flops 4259840 | bytes 6884672 | tf_op jit(solution)/shard_map/mul | solution.py:105
  69.1 1.3 %collective-permute-start.19 = (f32[80,4,128]{2,1,0:T(4,128)S(1)}, f32[80,4,128]{2,1,0:T(4,128)S(1)}, u32[]{:S(2)}, u32[]{:S(2)}) collective-permute-start(f32[80,4,128]{2,1,0:T(4,128)S(1)} %get-tuple-element.11), channel_id=1, source_target_pairs={{1,0},{3,2},{5,4},{7,6},{9,8},{11,10},{13,12},{15,14},{17,16},{19,... | collective-permute-start | bytes 491528 | tf_op jit(solution)/shard_map/ppermute | solution.py:22
  70.4 3.2 %collective-permute-start.18 = (f32[80,4,128]{2,1,0:T(4,128)S(1)}, f32[80,4,128]{2,1,0:T(4,128)S(1)}, u32[]{:S(2)}, u32[]{:S(2)}) collective-permute-start(f32[80,4,128]{2,1,0:T(4,128)S(1)} %get-tuple-element.12), channel_id=1, source_target_pairs={{0,1},{2,3},{4,5},{6,7},{8,9},{10,11},{12,13},{14,15},{16,17},{18,... | collective-permute-start | bytes 491528 | tf_op jit(solution)/shard_map/ppermute | solution.py:19
  74.4 2.3 %fusion.155 = f32[80,8,128]{2,1,0:T(8,128)S(1)} fusion(f32[80,8,128]{2,1,0:T(8,128)S(1)} %constant_dynamic-update-slice_fusion, f32[80,8,128]{2,1,0:T(8,128)S(1)} %fusion.182, f32[80,4,128]{2,1,0:T(4,128)S(1)} %collective-permute-done.8, f32[80,4,128]{2,1,0:T(4,128)S(1)} %collective-permute-done.9, f32[88,16,136]{2,1,0:T(8,128)S(1)} %select_maximum_fusion.10, ...), kind=kLoop, calls=%fused_computation.271 | loop fusion | flops 4423680 | bytes 6881820 | tf_op jit(solution)/shard_map/mul | solution.py:96
  76.8 1.3 %collective-permute-start.11 = (f32[80,4,128]{2,1,0:T(4,128)S(1)}, f32[80,4,128]{2,1,0:T(4,128)S(1)}, u32[]{:S(2)}, u32[]{:S(2)}) collective-permute-start(f32[80,4,128]{2,1,0:T(4,128)S(1)} %get-tuple-element.9), channel_id=1, source_target_pairs={{1,0},{3,2},{5,4},{7,6},{9,8},{11,10},{13,12},{15,14},{17,16},{19,... | collective-permute-start | bytes 491528 | tf_op jit(solution)/shard_map/ppermute | solution.py:22
  78.1 3.0 %collective-permute-start.10 = (f32[80,4,128]{2,1,0:T(4,128)S(1)}, f32[80,4,128]{2,1,0:T(4,128)S(1)}, u32[]{:S(2)}, u32[]{:S(2)}) collective-permute-start(f32[80,4,128]{2,1,0:T(4,128)S(1)} %get-tuple-element.10), channel_id=1, source_target_pairs={{0,1},{2,3},{4,5},{6,7},{8,9},{10,11},{12,13},{14,15},{16,17},{18,... | collective-permute-start | bytes 491528 | tf_op jit(solution)/shard_map/ppermute | solution.py:19
  82.9 8.1 %fusion.16 = f32[80,8,128]{2,1,0:T(8,128)} fusion(f32[80,8,128]{2,1,0:T(8,128)S(1)} %constant_dynamic-update-slice_fusion, f32[80,8,128]{2,1,0:T(8,128)S(1)} %fusion.43, f32[80,8,128]{2,1,0:T(8,128)} %copy-done, f32[80,4,128]{2,1,0:T(4,128)} %copy-done.3, f32[80,4,128]{2,1,0:T(4,128)S(1)} %collective-permute-done.19, f32[80,4,128]{2,1,0:T(4,128)} %copy-done.5, ...), kind=kLoop, calls=%fused_computation.132 | loop fusion | flops 9748480 | bytes 14093852 | tf_op jit(solution)/shard_map/add | solution.py:107
  93.2 5.5 %collective-permute-start.23 = (f32[16,8,128]{2,1,0:T(8,128)S(1)}, f32[16,8,128]{2,1,0:T(8,128)S(1)}, u32[]{:S(2)}, u32[]{:S(2)}) collective-permute-start(f32[16,8,128]{2,1,0:T(8,128)S(1)} %get-tuple-element.6), channel_id=1, source_target_pairs={{0,8},{4,12},{1,9},{5,13},{2,10},{6,14},{3,11},{7,15},{16,24},{20,... | collective-permute-start | bytes 196616 | tf_op jit(solution)/shard_map/ppermute | solution.py:30
  98.7 1.3 %collective-permute-start.22 = (f32[16,8,128]{2,1,0:T(8,128)S(1)}, f32[16,8,128]{2,1,0:T(8,128)S(1)}, u32[]{:S(2)}, u32[]{:S(2)}) collective-permute-start(f32[16,8,128]{2,1,0:T(8,128)S(1)} %get-tuple-element.7), channel_id=1, source_target_pairs={{0,4},{4,8},{8,12},{1,5},{5,9},{9,13},{2,6},{6,10},{10,14},{3,7},{... | collective-permute-start | bytes 196616 | tf_op jit(solution)/shard_map/ppermute | solution.py:30
  101.9 4.3 %collective-permute-done.21 = f32[16,8,128]{2,1,0:T(8,128)S(1)} collective-permute-done((f32[16,8,128]{2,1,0:T(8,128)S(1)}, f32[16,8,128]{2,1,0:T(8,128)S(1)}, u32[]{:S(2)}, u32[]{:S(2)}) %collective-permute-start.21) | collective-permute-done | bytes 65568 | tf_op jit(solution)/shard_map/ppermute | solution.py:30
  108.6 9.2 %reduce-scatter.4.cloned.1.call-done = f32[64,128]{1,0:T(8,128)} async-done(((f32[128,128]{1,0:T(8,128)}), f32[64,128]{1,0:T(8,128)}) %reduce-scatter.4.cloned.1.call-update) | async-done | bytes 32784
  (94 shorter events, 20.4 us)
Async XLA Ops:
  6.5 18.6 %copy-start.9 = (s32[1,3]{1,0:T(1,128)S(1)}, s32[1,3]{1,0:T(1,128)}, u32[]{:S(2)}) copy-start(s32[1,3]{1,0:T(1,128)} %param.12) | copy-start | bytes 40
  6.5 20.6 %copy-start.8 = (f32[1,4]{1,0:T(1,128)S(1)}, f32[1,4]{1,0:T(1,128)}, u32[]{:S(2)}) copy-start(f32[1,4]{1,0:T(1,128)} %param.11) | copy-start | bytes 52
  6.5 21.2 %copy-start.10 = (s32[1,80,8]{1,2,0:T(8,128)S(1)}, s32[1,80,8]{1,2,0:T(8,128)}, u32[]{:S(2)}) copy-start(s32[1,80,8]{1,2,0:T(8,128)} %param.14) | copy-start | bytes 7684
  6.5 21.2 %copy-start.7 = (f32[1,4,80,8]{2,3,1,0:T(8,128)S(1)}, f32[1,4,80,8]{2,3,1,0:T(8,128)}, u32[]{:S(2)}) copy-start(f32[1,4,80,8]{2,3,1,0:T(8,128)} %param.15) | copy-start | bytes 30724
  6.5 111.3 %reduce-scatter.4.cloned.1.call-start = ((), (), s32[]{:S(2)}) async-start(), calls=%async_computation.1 | async-start | bytes 98304
  6.6 29.9 %collective-permute-start.3 = (f32[16,8,128]{2,1,0:T(8,128)}, f32[16,8,128]{2,1,0:T(8,128)S(1)}, u32[]{:S(2)}, u32[]{:S(2)}) collective-permute-start(f32[16,8,128]{2,1,0:T(8,128)} %bitcast.49), channel_id=1, source_target_pairs={{8,0},{12,4},{9,1},{13,5},{10,2},{14,6},{11,3},{15,7},{24,16},{28,... | collective-permute-start | bytes 196616 | tf_op jit(solution)/shard_map/ppermute | solution.py:30
  8.0 25.4 %collective-permute-start.2 = (f32[16,8,128]{2,1,0:T(8,128)}, f32[16,8,128]{2,1,0:T(8,128)S(1)}, u32[]{:S(2)}, u32[]{:S(2)}) collective-permute-start(f32[16,8,128]{2,1,0:T(8,128)} %bitcast.50), channel_id=1, source_target_pairs={{4,0},{8,4},{12,8},{5,1},{9,5},{13,9},{6,2},{10,6},{14,10},{7,3},{... | collective-permute-start | bytes 196616 | tf_op jit(solution)/shard_map/ppermute | solution.py:30
  9.3 22.7 %collective-permute-start.1 = (f32[16,8,128]{2,1,0:T(8,128)}, f32[16,8,128]{2,1,0:T(8,128)S(1)}, u32[]{:S(2)}, u32[]{:S(2)}) collective-permute-start(f32[16,8,128]{2,1,0:T(8,128)} %bitcast.51), channel_id=1, source_target_pairs={{0,4},{4,8},{8,12},{1,5},{5,9},{9,13},{2,6},{6,10},{10,14},{3,7},{... | collective-permute-start | bytes 196616 | tf_op jit(solution)/shard_map/ppermute | solution.py:30
  14.9 14.1 %collective-permute-start = (f32[16,8,128]{2,1,0:T(8,128)}, f32[16,8,128]{2,1,0:T(8,128)S(1)}, u32[]{:S(2)}, u32[]{:S(2)}) collective-permute-start(f32[16,8,128]{2,1,0:T(8,128)} %bitcast.52), channel_id=1, source_target_pairs={{0,8},{4,12},{1,9},{5,13},{2,10},{6,14},{3,11},{7,15},{16,24},{20,... | collective-permute-start | bytes 196616 | tf_op jit(solution)/shard_map/ppermute | solution.py:30
  22.5 10.9 %copy-start.6 = (f32[1,16,8,128]{3,2,1,0:T(8,128)S(1)}, f32[1,16,8,128]{3,2,1,0:T(8,128)}, u32[]{:S(2)}) copy-start(f32[1,16,8,128]{3,2,1,0:T(8,128)} %param.8) | copy-start | bytes 196612
  23.9 20.6 %collective-permute-start.5 = (f32[80,4,128]{2,1,0:T(4,128)S(1)}, f32[80,4,128]{2,1,0:T(4,128)S(1)}, u32[]{:S(2)}, u32[]{:S(2)}) collective-permute-start(f32[80,4,128]{2,1,0:T(4,128)S(1)} %get-tuple-element.17), channel_id=1, source_target_pairs={{1,0},{3,2},{5,4},{7,6},{9,8},{11,10},{13,12},{15,14},{17,16},{19,... | collective-permute-start | bytes 491528 | tf_op jit(solution)/shard_map/ppermute | solution.py:22
  28.2 10.0 %copy-start.2 = (bf16[1,2,80,8,128]{4,3,2,1,0:T(8,128)(2,1)S(1)}, bf16[1,2,80,8,128]{4,3,2,1,0:T(8,128)(2,1)}, u32[]{:S(2)}) copy-start(bf16[1,2,80,8,128]{4,3,2,1,0:T(8,128)(2,1)} %param.10) | copy-start | bytes 983044
  28.9 15.5 %collective-permute-start.4 = (f32[80,4,128]{2,1,0:T(4,128)S(1)}, f32[80,4,128]{2,1,0:T(4,128)S(1)}, u32[]{:S(2)}, u32[]{:S(2)}) collective-permute-start(f32[80,4,128]{2,1,0:T(4,128)S(1)} %get-tuple-element.18), channel_id=1, source_target_pairs={{0,1},{2,3},{4,5},{6,7},{8,9},{10,11},{12,13},{14,15},{16,17},{18,... | collective-permute-start | bytes 491528 | tf_op jit(solution)/shard_map/ppermute | solution.py:19
  32.0 4.4 %collective-permute-start.13 = (f32[80,4,128]{2,1,0:T(4,128)S(1)}, f32[80,4,128]{2,1,0:T(4,128)S(1)}, u32[]{:S(2)}, u32[]{:S(2)}) collective-permute-start(f32[80,4,128]{2,1,0:T(4,128)S(1)} %get-tuple-element.23), channel_id=1, source_target_pairs={{1,0},{3,2},{5,4},{7,6},{9,8},{11,10},{13,12},{15,14},{17,16},{19,... | collective-permute-start | bytes 491528 | tf_op jit(solution)/shard_map/ppermute | solution.py:22
  33.4 4.1 %collective-permute-start.12 = (f32[80,4,128]{2,1,0:T(4,128)S(1)}, f32[80,4,128]{2,1,0:T(4,128)S(1)}, u32[]{:S(2)}, u32[]{:S(2)}) collective-permute-start(f32[80,4,128]{2,1,0:T(4,128)S(1)} %get-tuple-element.24), channel_id=1, source_target_pairs={{0,1},{2,3},{4,5},{6,7},{8,9},{10,11},{12,13},{14,15},{16,17},{18,... | collective-permute-start | bytes 491528 | tf_op jit(solution)/shard_map/ppermute | solution.py:19
  40.0 12.1 %collective-permute-start.15 = (f32[80,4,128]{2,1,0:T(4,128)S(1)}, f32[80,4,128]{2,1,0:T(4,128)S(1)}, u32[]{:S(2)}, u32[]{:S(2)}) collective-permute-start(f32[80,4,128]{2,1,0:T(4,128)S(1)} %get-tuple-element.21), channel_id=1, source_target_pairs={{1,0},{3,2},{5,4},{7,6},{9,8},{11,10},{13,12},{15,14},{17,16},{19,... | collective-permute-start | bytes 491528 | tf_op jit(solution)/shard_map/ppermute | solution.py:22
  41.4 10.7 %collective-permute-start.14 = (f32[80,4,128]{2,1,0:T(4,128)S(1)}, f32[80,4,128]{2,1,0:T(4,128)S(1)}, u32[]{:S(2)}, u32[]{:S(2)}) collective-permute-start(f32[80,4,128]{2,1,0:T(4,128)S(1)} %get-tuple-element.22), channel_id=1, source_target_pairs={{0,1},{2,3},{4,5},{6,7},{8,9},{10,11},{12,13},{14,15},{16,17},{18,... | collective-permute-start | bytes 491528 | tf_op jit(solution)/shard_map/ppermute | solution.py:19
  47.7 11.2 %collective-permute-start.7 = (f32[80,4,128]{2,1,0:T(4,128)S(1)}, f32[80,4,128]{2,1,0:T(4,128)S(1)}, u32[]{:S(2)}, u32[]{:S(2)}) collective-permute-start(f32[80,4,128]{2,1,0:T(4,128)S(1)} %get-tuple-element.15), channel_id=1, source_target_pairs={{1,0},{3,2},{5,4},{7,6},{9,8},{11,10},{13,12},{15,14},{17,16},{19,... | collective-permute-start | bytes 491528 | tf_op jit(solution)/shard_map/ppermute | solution.py:22
  49.0 10.0 %collective-permute-start.6 = (f32[80,4,128]{2,1,0:T(4,128)S(1)}, f32[80,4,128]{2,1,0:T(4,128)S(1)}, u32[]{:S(2)}, u32[]{:S(2)}) collective-permute-start(f32[80,4,128]{2,1,0:T(4,128)S(1)} %get-tuple-element.16), channel_id=1, source_target_pairs={{0,1},{2,3},{4,5},{6,7},{8,9},{10,11},{12,13},{14,15},{16,17},{18,... | collective-permute-start | bytes 491528 | tf_op jit(solution)/shard_map/ppermute | solution.py:19
  54.6 11.9 %collective-permute-start.17 = (f32[80,4,128]{2,1,0:T(4,128)S(1)}, f32[80,4,128]{2,1,0:T(4,128)S(1)}, u32[]{:S(2)}, u32[]{:S(2)}) collective-permute-start(f32[80,4,128]{2,1,0:T(4,128)S(1)} %get-tuple-element.19), channel_id=1, source_target_pairs={{1,0},{3,2},{5,4},{7,6},{9,8},{11,10},{13,12},{15,14},{17,16},{19,... | collective-permute-start | bytes 491528 | tf_op jit(solution)/shard_map/ppermute | solution.py:22
  55.9 10.7 %collective-permute-start.16 = (f32[80,4,128]{2,1,0:T(4,128)S(1)}, f32[80,4,128]{2,1,0:T(4,128)S(1)}, u32[]{:S(2)}, u32[]{:S(2)}) collective-permute-start(f32[80,4,128]{2,1,0:T(4,128)S(1)} %get-tuple-element.20), channel_id=1, source_target_pairs={{0,1},{2,3},{4,5},{6,7},{8,9},{10,11},{12,13},{14,15},{16,17},{18,... | collective-permute-start | bytes 491528 | tf_op jit(solution)/shard_map/ppermute | solution.py:19
  62.2 11.4 %collective-permute-start.9 = (f32[80,4,128]{2,1,0:T(4,128)S(1)}, f32[80,4,128]{2,1,0:T(4,128)S(1)}, u32[]{:S(2)}, u32[]{:S(2)}) collective-permute-start(f32[80,4,128]{2,1,0:T(4,128)S(1)} %get-tuple-element.13), channel_id=1, source_target_pairs={{1,0},{3,2},{5,4},{7,6},{9,8},{11,10},{13,12},{15,14},{17,16},{19,... | collective-permute-start | bytes 491528 | tf_op jit(solution)/shard_map/ppermute | solution.py:22
  63.5 10.1 %collective-permute-start.8 = (f32[80,4,128]{2,1,0:T(4,128)S(1)}, f32[80,4,128]{2,1,0:T(4,128)S(1)}, u32[]{:S(2)}, u32[]{:S(2)}) collective-permute-start(f32[80,4,128]{2,1,0:T(4,128)S(1)} %get-tuple-element.14), channel_id=1, source_target_pairs={{0,1},{2,3},{4,5},{6,7},{8,9},{10,11},{12,13},{14,15},{16,17},{18,... | collective-permute-start | bytes 491528 | tf_op jit(solution)/shard_map/ppermute | solution.py:19
  69.1 12.1 %collective-permute-start.19 = (f32[80,4,128]{2,1,0:T(4,128)S(1)}, f32[80,4,128]{2,1,0:T(4,128)S(1)}, u32[]{:S(2)}, u32[]{:S(2)}) collective-permute-start(f32[80,4,128]{2,1,0:T(4,128)S(1)} %get-tuple-element.11), channel_id=1, source_target_pairs={{1,0},{3,2},{5,4},{7,6},{9,8},{11,10},{13,12},{15,14},{17,16},{19,... | collective-permute-start | bytes 491528 | tf_op jit(solution)/shard_map/ppermute | solution.py:22
  70.4 10.8 %collective-permute-start.18 = (f32[80,4,128]{2,1,0:T(4,128)S(1)}, f32[80,4,128]{2,1,0:T(4,128)S(1)}, u32[]{:S(2)}, u32[]{:S(2)}) collective-permute-start(f32[80,4,128]{2,1,0:T(4,128)S(1)} %get-tuple-element.12), channel_id=1, source_target_pairs={{0,1},{2,3},{4,5},{6,7},{8,9},{10,11},{12,13},{14,15},{16,17},{18,... | collective-permute-start | bytes 491528 | tf_op jit(solution)/shard_map/ppermute | solution.py:19
  76.7 6.2 %copy-start = (f32[80,8,128]{2,1,0:T(8,128)}, f32[80,8,128]{2,1,0:T(8,128)S(1)}, u32[]{:S(2)}) copy-start(f32[80,8,128]{2,1,0:T(8,128)S(1)} %fusion.155) | copy-start | bytes 983044
  76.8 5.1 %collective-permute-start.11 = (f32[80,4,128]{2,1,0:T(4,128)S(1)}, f32[80,4,128]{2,1,0:T(4,128)S(1)}, u32[]{:S(2)}, u32[]{:S(2)}) collective-permute-start(f32[80,4,128]{2,1,0:T(4,128)S(1)} %get-tuple-element.9), channel_id=1, source_target_pairs={{1,0},{3,2},{5,4},{7,6},{9,8},{11,10},{13,12},{15,14},{17,16},{19,... | collective-permute-start | bytes 491528 | tf_op jit(solution)/shard_map/ppermute | solution.py:22
  78.1 4.1 %collective-permute-start.10 = (f32[80,4,128]{2,1,0:T(4,128)S(1)}, f32[80,4,128]{2,1,0:T(4,128)S(1)}, u32[]{:S(2)}, u32[]{:S(2)}) collective-permute-start(f32[80,4,128]{2,1,0:T(4,128)S(1)} %get-tuple-element.10), channel_id=1, source_target_pairs={{0,1},{2,3},{4,5},{6,7},{8,9},{10,11},{12,13},{14,15},{16,17},{18,... | collective-permute-start | bytes 491528 | tf_op jit(solution)/shard_map/ppermute | solution.py:19
  91.9 9.4 %collective-permute-start.20 = (f32[16,8,128]{2,1,0:T(8,128)S(1)}, f32[16,8,128]{2,1,0:T(8,128)S(1)}, u32[]{:S(2)}, u32[]{:S(2)}) collective-permute-start(f32[16,8,128]{2,1,0:T(8,128)S(1)} %get-tuple-element.5), channel_id=1, source_target_pairs={{8,0},{12,4},{9,1},{13,5},{10,2},{14,6},{11,3},{15,7},{24,16},{28,... | collective-permute-start | bytes 196616 | tf_op jit(solution)/shard_map/ppermute | solution.py:30
  93.2 8.1 %collective-permute-start.23 = (f32[16,8,128]{2,1,0:T(8,128)S(1)}, f32[16,8,128]{2,1,0:T(8,128)S(1)}, u32[]{:S(2)}, u32[]{:S(2)}) collective-permute-start(f32[16,8,128]{2,1,0:T(8,128)S(1)} %get-tuple-element.6), channel_id=1, source_target_pairs={{0,8},{4,12},{1,9},{5,13},{2,10},{6,14},{3,11},{7,15},{16,24},{20,... | collective-permute-start | bytes 196616 | tf_op jit(solution)/shard_map/ppermute | solution.py:30
  98.7 3.2 %collective-permute-start.22 = (f32[16,8,128]{2,1,0:T(8,128)S(1)}, f32[16,8,128]{2,1,0:T(8,128)S(1)}, u32[]{:S(2)}, u32[]{:S(2)}) collective-permute-start(f32[16,8,128]{2,1,0:T(8,128)S(1)} %get-tuple-element.7), channel_id=1, source_target_pairs={{0,4},{4,8},{8,12},{1,5},{5,9},{9,13},{2,6},{6,10},{10,14},{3,7},{... | collective-permute-start | bytes 196616 | tf_op jit(solution)/shard_map/ppermute | solution.py:30
  100.0 6.2 %collective-permute-start.21 = (f32[16,8,128]{2,1,0:T(8,128)S(1)}, f32[16,8,128]{2,1,0:T(8,128)S(1)}, u32[]{:S(2)}, u32[]{:S(2)}) collective-permute-start(f32[16,8,128]{2,1,0:T(8,128)S(1)} %get-tuple-element.8), channel_id=1, source_target_pairs={{4,0},{8,4},{12,8},{5,1},{9,5},{13,9},{6,2},{10,6},{14,10},{7,3},{... | collective-permute-start | bytes 196616 | tf_op jit(solution)/shard_map/ppermute | solution.py:30
  (4 other events, 7.9 us)
Sparse Core Ops, SparseCore 0:
  108.7 9.0 reduce-scatter.3
where the time goes:
time: 127 us
  starting transfers between devices  57.6 us (45%)
  other arithmetic  30.2 us (24%)
  between operations  16.1 us (13%)
  waiting for transfers between devices  15.2 us (12%)
  local copies, waits for them, and re-layouts  7.44 us (6%)
    ppermute x8, starting transfers between devices, with_halo(): lax.ppermute(lax.slice_in_dim(block, block.shape[dim] - width, None, axis...  24.5 us
    ppermute x8, starting transfers between devices, passed_along(): return lax.ppermute(value, axis, pairs)  22.6 us
    ppermute x8, starting transfers between devices, with_halo(): lax.ppermute(lax.slice_in_dim(block, 0, width, axis=dim), axis, backward)  10.5 us
    unnamed x2, waiting for transfers between devices  9.22 us
    add x1, other arithmetic, shards(): partial_value = partial_value + stored[later] * a_now  8.05 us
    mul x3, other arithmetic, shards(): keep * (2.0 * f_now - f_prev + window * laplace_rims(f_now) + wav[step] *...  7.14 us
    concatenate x8, other arithmetic, with_halo(): block = jnp.concatenate([low, block, high], axis=dim)  5.98 us
    mul x3, other arithmetic, shards(): keep * (2.0 * a_now - a_next + window * laplace_rims(a_now) + inject)  5.05 us
  transfers between devices with their start and end apart: 25, of which 5 were waited for; matrix products, arithmetic and copies ran while one was open for 19% of the time, Pallas kernels for 0%

commit v1 on v0

v1 whole, which is shorter than its diff:
```python
import functools

import jax
import jax.numpy as jnp
from jax import lax
from jax.experimental import pallas as pl
from jax.experimental.pallas import tpu as pltpu
from jax.sharding import PartitionSpec as P

R = 2
STEPS = 4
NB = 2 * R + 1
MESH = pl.DeviceIdType.MESH

coeffs = (-205.0 / 72.0, 8.0 / 5.0, -1.0 / 5.0, 8.0 / 315.0, -1.0 / 560.0)
image_scale = 0.05
f32 = jnp.float32
bf16 = jnp.bfloat16


def kernel(nblock, nshot, vel, fwd, adj, wav, src, ap, mask, rec, out,
           F, A, W, ZF, ZA, PV, O, T, B, G, S, H,
           vs, vr, fs, fr, as_, ar, gs, gr, ss, sr):
    bx, bys, bz = vel.shape
    home = lax.axis_index("block")
    team = lax.axis_index("shot")
    sub = lax.axis_index("sub")
    lo = jnp.maximum(R - home, 0)
    hi = jnp.minimum(R + nblock - home, NB)
    offsets = [o for o in range(-R, R + 1) if o != 0]

    def near(o):
        return (home + o >= 0) & (home + o < nblock)

    barrier = pltpu.get_barrier_semaphore()
    for o in offsets:
        @pl.when(near(o))
        def _():
            pl.semaphore_signal(barrier, inc=1, device_id={"block": home + o}, device_id_type=MESH)
    for r in range(1, nshot):
        pl.semaphore_signal(barrier, inc=1, device_id={"shot": lax.rem(team + r, nshot)}, device_id_type=MESH)
    pl.semaphore_signal(barrier, inc=1, device_id={"sub": 1 - sub}, device_id_type=MESH)

    def keep_of(b):
        return jnp.where((b >= R - ap[0, 0]) & (b <= R + ap[0, 1]), 1.0, 0.0).astype(f32)

    def at(field, t, b):
        return field[t, pl.ds(4 + b * bx, bx), 8:16, :]

    zx = jnp.zeros((4, 8, bz), f32)

    @pl.when(sub == 0)
    def _():
        lax.fori_loop(lo, hi, functools.partial(clear_at, F, A, 0, bx, bz), 0)

    @pl.when(sub == 1)
    def _():
        lax.fori_loop(lo, hi, functools.partial(clear_at, F, A, 16, bx, bz), 0)

    for field in (F, A):
        for t in range(STEPS):
            field[t, pl.ds(lo * bx, 4), 8:16, :] = zx
            field[t, pl.ds(4 + hi * bx, 4), 8:16, :] = zx

    def load_states(b, c):
        kb = keep_of(b)
        rows = pl.ds(4 + b * bx, bx)
        F[0, rows, 8:16, :] = kb * fwd[1, pl.ds(b * bx, bx)].astype(f32)
        A[0, rows, 8:16, :] = kb * adj[1, pl.ds(b * bx, bx)].astype(f32)
        return c

    lax.fori_loop(lo, hi, load_states, 0)

    count = (hi - lo - 1) + (nshot - 1) + 1
    pl.semaphore_wait(barrier, count)

    def vel_copy(o):
        j = R - o
        return pltpu.make_async_remote_copy(
            src_ref=vel, dst_ref=W.at[pl.ds(j * bx, bx)], send_sem=vs.at[j], recv_sem=vr.at[j],
            device_id={"block": home + o}, device_id_type=MESH)

    def rim_copy(field, t, ssem, rsem):
        x = NB * bx
        return pltpu.make_async_remote_copy(
            src_ref=field.at[t, pl.ds(4, x), pl.ds(8, 8), :],
            dst_ref=field.at[t, pl.ds(4, x), pl.ds(pl.multiple_of(16 * sub, 8), 8), :],
            send_sem=ssem.at[t], recv_sem=rsem.at[t],
            device_id={"sub": 1 - sub}, device_id_type=MESH)

    rim_copy(F, 0, fs, fr).start()
    rim_copy(A, 0, as_, ar).start()
    for o in (-2, 2, -1, 1):
        @pl.when(near(o))
        def _():
            vel_copy(o).start()

    i0 = lax.broadcasted_iota(jnp.int32, (bz, bz), 0)
    i1 = lax.broadcasted_iota(jnp.int32, (bz, bz), 1)
    dist = jnp.abs(i0 - i1)
    band = jnp.where(dist == 0, 3.0 * coeffs[0], 0.0).astype(f32)
    for j in range(1, 5):
        band = jnp.where(dist == j, coeffs[j], band)
    band_hi = band.astype(bf16)
    band_lo = (band - band_hi.astype(f32)).astype(bf16)
    B[0:bz, 0:bz] = band_hi
    B[bz:2 * bz, 0:bz] = band_hi
    B[0:bz, bz:2 * bz] = band_lo
    B[bz:2 * bz, bz:2 * bz] = jnp.zeros((bz, bz), bf16)

    ox = lax.broadcasted_iota(jnp.int32, (bx, bys, bz), 0)
    oy = lax.broadcasted_iota(jnp.int32, (bx, bys, bz), 1) + sub * bys
    oz = lax.broadcasted_iota(jnp.int32, (bx, bys, bz), 2)
    O[...] = jnp.where((ox == src[0, 0]) & (oy == src[0, 1]) & (oz == src[0, 2]), 1.0, 0.0).astype(f32)
    live = mask[...].astype(f32)
    T[...] = jnp.zeros_like(T)
    for t in range(STEPS):
        T[t, :, 0:NB * bx] = (live * rec[t]).T
    surface = lax.broadcasted_iota(jnp.int32, (bys, bz), 1) == 0

    W[R * bx:(R + 1) * bx] = vel[...]

    def laplace(field, t, b):
        own = at(field, t, b)
        flat = own.reshape(bx * bys, bz)
        high = flat.astype(bf16)
        low = (flat - high.astype(f32)).astype(bf16)
        both = jnp.concatenate([high, low], axis=1)
        prod = jnp.dot(both, B[...], preferred_element_type=f32)
        total = (prod[:, :bz] + prod[:, bz:]).reshape(bx, bys, bz)
        for j in range(1, 5):
            near_sum = (field[t, pl.ds(4 + j + b * bx, bx), 8:16, :] + field[t, pl.ds(4 - j + b * bx, bx), 8:16, :]
                        + field[t, pl.ds(4 + b * bx, bx), 8 + j:16 + j, :] + field[t, pl.ds(4 + b * bx, bx), 8 - j:16 - j, :])
            total = total + coeffs[j] * near_sum
        return own, total

    def source_term(step, b):
        amp = jnp.where(b == R, wav[0, step], 0.0)
        return amp * O[...]

    def receiver_term(step, b):
        row = pltpu.roll(T[STEPS - 1 - step], 128 - b * bx, 1) * keep_of(b)
        parts = []
        for x in range(bx):
            moved = pltpu.roll(row, 128 - x, 1) if x else row
            parts.append(jnp.where(surface, moved, 0.0)[None])
        return jnp.concatenate(parts, axis=0)

    rim_copy(F, 0, fs, fr).wait_recv()
    rim_copy(A, 0, as_, ar).wait_recv()

    def first_diff(b, c):
        cells = pl.ds(b * bx, bx)
        ZF[cells] = laplace(F, 0, b)[1]
        ZA[cells] = laplace(A, 0, b)[1]
        return c

    lax.fori_loop(lo, hi, first_diff, 0)
    for o in offsets:
        @pl.when(near(o))
        def _():
            vel_copy(-o).wait_recv()

    def first_f(b, c):
        kb = keep_of(b)
        cells = pl.ds(b * bx, bx)
        w = kb * W[cells]
        W[cells] = w
        F[1, pl.ds(4 + b * bx, bx), 8:16, :] = (
            2.0 * at(F, 0, b) - kb * fwd[0, cells].astype(f32) + w * ZF[cells] + source_term(0, b))
        return c

    lax.fori_loop(lo, hi, first_f, 0)
    rim_copy(F, 1, fs, fr).start()

    def first_a(b, c):
        cells = pl.ds(b * bx, bx)
        A[1, pl.ds(4 + b * bx, bx), 8:16, :] = (
            2.0 * at(A, 0, b) - keep_of(b) * adj[0, cells].astype(f32) + W[cells] * ZA[cells] + receiver_term(0, b))
        return c

    lax.fori_loop(lo, hi, first_a, 0)
    rim_copy(A, 1, as_, ar).start()

    def image_copy(j):
        return pltpu.make_async_remote_copy(
            src_ref=PV.at[pl.ds(j * bx, bx)], dst_ref=G.at[j], send_sem=gs.at[j], recv_sem=gr.at[j],
            device_id={"block": home + j - R}, device_id_type=MESH)

    for step in range(1, STEPS):
        last = step == STEPS - 1
        rim_copy(F, step, fs, fr).wait_recv()

        def f_block(b, c):
            cells = pl.ds(b * bx, bx)
            own, lap = laplace(F, step, b)
            new = 2.0 * own - at(F, step - 1, b) + W[cells] * lap + source_term(step, b)
            if not last:
                F[step + 1, pl.ds(4 + b * bx, bx), 8:16, :] = new
            if step + 1 > 2:
                PV[cells] = PV[cells] + new * at(A, STEPS - step - 1, b)
            return c

        lax.fori_loop(lo, hi, f_block, 0)
        if not last:
            rim_copy(F, step + 1, fs, fr).start()
        rim_copy(A, step, as_, ar).wait_recv()

        def a_block(b, c):
            cells = pl.ds(b * bx, bx)
            own, lap = laplace(A, step, b)
            new = 2.0 * own - at(A, step - 1, b) + W[cells] * lap + receiver_term(step, b)
            if not last:
                A[step + 1, pl.ds(4 + b * bx, bx), 8:16, :] = new
            if step == 1:
                PV[cells] = at(F, 2, b) * new
            else:
                PV[cells] = PV[cells] + at(F, STEPS - step - 1, b) * new
            if last:
                @pl.when(b != R)
                def _():
                    image_copy(b).start()
            return c

        lax.fori_loop(lo, hi, a_block, 0)
        if not last:
            rim_copy(A, step + 1, as_, ar).start()

    H[...] = PV[R * bx:(R + 1) * bx]
    for o in (-1, 1, -2, 2):
        @pl.when(near(o))
        def _():
            j = R - o
            image_copy(j).wait_recv()
            H[...] = H[...] + G[j]

    zl = bz // nshot
    xg = bx // nshot
    lane = lax.broadcasted_iota(jnp.int32, (xg, bys, bz), 2)

    def packed(d):
        total = jnp.zeros((xg, bys, bz), f32)
        for k in range(nshot):
            shift = lax.rem((k - d + nshot) * zl, bz)
            moved = pltpu.roll(H[k * xg:(k + 1) * xg].reshape(xg * bys, bz), shift, 1).reshape(xg, bys, bz)
            total = jnp.where((lane >= k * zl) & (lane < (k + 1) * zl), moved, total)
        return total

    def team_copy(r):
        return pltpu.make_async_remote_copy(
            src_ref=S.at[r], dst_ref=S.at[nshot + r], send_sem=ss.at[r], recv_sem=sr.at[r],
            device_id={"shot": lax.rem(team + r, nshot)}, device_id_type=MESH)

    for r in range(1, nshot):
        S[r] = packed(lax.rem(team + r, nshot))
        team_copy(r).start()
    total = packed(team)
    for r in range(1, nshot):
        team_copy(r).wait_recv()
        total = total + S[nshot + r]
    out[...] = image_scale * total

    for t in range(STEPS):
        rim_copy(F, t, fs, fr).wait_send()
        rim_copy(A, t, as_, ar).wait_send()
    for o in offsets:
        @pl.when(near(o))
        def _():
            vel_copy(o).wait_send()
            image_copy(R + o).wait_send()
    for r in range(1, nshot):
        team_copy(r).wait_send()


def clear_at(F, A, row, bx, bz, b, c):
    for field in (F, A):
        for t in range(STEPS):
            field[t, pl.ds(4 + b * bx, bx), row:row + 8, :] = jnp.zeros((bx, 8, bz), f32)
    return c


def shards(nblock, nshot, vel_sq, fwd_state, adj_state, wavelet, source, aperture, rec_mask, rec_data):
    bx, bys, bz = vel_sq.shape[1:]
    width = NB * bx
    vmem = pl.BlockSpec(memory_space=pltpu.VMEM)
    smem = pl.BlockSpec(memory_space=pltpu.SMEM)
    dma = pltpu.SemaphoreType.DMA
    packed = pl.pallas_call(
        functools.partial(kernel, nblock, nshot),
        out_shape=jax.ShapeDtypeStruct((bx // nshot, bys, bz), f32),
        in_specs=[vmem, vmem, vmem, smem, smem, smem, vmem, vmem],
        out_specs=vmem,
        scratch_shapes=[
            pltpu.VMEM((STEPS, width + 8, 24, bz), f32),
            pltpu.VMEM((STEPS, width + 8, 24, bz), f32),
            pltpu.VMEM((width, bys, bz), f32),
            pltpu.VMEM((width, bys, bz), f32),
            pltpu.VMEM((width, bys, bz), f32),
            pltpu.VMEM((width, bys, bz), f32),
            pltpu.VMEM((bx, bys, bz), f32),
            pltpu.VMEM((STEPS, bys, bz), f32),
            pltpu.VMEM((2 * bz, 2 * bz), bf16),
            pltpu.VMEM((NB, bx, bys, bz), f32),
            pltpu.VMEM((2 * nshot, bx // nshot, bys, bz), f32),
            pltpu.VMEM((bx, bys, bz), f32),
            dma((NB,)), dma((NB,)),
            dma((STEPS,)), dma((STEPS,)),
            dma((STEPS,)), dma((STEPS,)),
            dma((NB,)), dma((NB,)),
            dma((nshot,)), dma((nshot,)),
        ],
        compiler_params=pltpu.CompilerParams(
            collective_id=0, has_side_effects=True, vmem_limit_bytes=40 * 1024 * 1024),
    )(vel_sq[0], fwd_state[0], adj_state[0], wavelet, source, aperture, rec_mask[0], rec_data[0])
    zl = bz // nshot
    image = packed.reshape(bx // nshot, bys, nshot, zl).transpose(2, 0, 1, 3)
    return image.reshape(1, bx, bys, zl)


def solution(mesh):
    placed = (
        P(("parts", "block"), None, "sub", None),
        P(("parts", "block", "shot"), None, None, "sub", None),
        P(("parts", "block", "shot"), None, None, "sub", None),
        P(("parts", "block", "shot"), None),
        P(("parts", "block", "shot"), None),
        P(("parts", "block", "shot"), None),
        P(("parts", "block", "shot"), None, "sub"),
        P(("parts", "block", "shot"), None, None, "sub"),
    )
    return jax.shard_map(
        functools.partial(shards, mesh.shape["block"], mesh.shape["shot"]),
        mesh=mesh,
        in_specs=placed,
        out_specs=P(("parts", "block"), None, "sub", "shot"),
        check_vma=False,
    )
```

time: 127 us -> 31 us (0.24)
  starting transfers between devices: 57.6 us -> 0 us
  other arithmetic: 30.2 us -> 0 us
  Pallas kernels: 0 us -> 25.7 us
  between operations: 16.1 us -> 0.06 us
  waiting for transfers between devices: 15.2 us -> 0 us
  local copies, waits for them, and re-layouts: 7.44 us -> 4.89 us
    ppermute x24 -> x0, starting transfers between devices: 57.6 us -> none  [the longest x8 24.5 us: with_halo(): lax.ppermute(lax.slice_in_dim(block, block.shape[dim] - width, None, axis...]
    pallas_call x0 -> x1, Pallas kernels: none -> 25.7 us  [shards(): pl.pallas_call(functools.partial(kernel, nblock, nshot), out_shape=jax.Sh...]
    mul x9 -> x0, other arithmetic: 13.3 us -> none  [the longest x3 7.14 us: shards(): keep * (2.0 * f_now - f_prev + window * laplace_rims(f_now) + wav[step] *...]
    unnamed x2 -> x0, waiting for transfers between devices: 9.22 us -> none
    add x2 -> x0, other arithmetic: 8.92 us -> none  [the longest x1 8.05 us: shards(): partial_value = partial_value + stored[later] * a_now]
    ppermute x24 -> x0, waiting for transfers between devices: 6.03 us -> none  [the longest x8 4.85 us: passed_along(): return lax.ppermute(value, axis, pairs)]
    concatenate x8 -> x0, other arithmetic: 5.98 us -> none  [with_halo(): block = jnp.concatenate([low, block, high], axis=dim)]
    slice x12 -> x0, local copies, waits for them, and re-layouts: 4 us -> none  [the longest x1 1.34 us: shards(): ap[0]]
  transfers between devices with their start and end apart: 25 -> 0, of which waited for: 5 -> 0; matrix products, arithmetic and copies ran while one was open for 19% -> 0% of each run, Pallas kernels for 0% -> 0%
where the time goes in v1:
time: 31 us; the launch traced here: 30.7 us
  Pallas kernels  25.7 us (83%)
  local copies, waits for them, and re-layouts  4.89 us (16%)
    pallas_call x1, Pallas kernels, shards(): pl.pallas_call(functools.partial(kernel, nblock, nshot), out_shape=jax.Sh...  25.7 us
    unnamed x18, local copies, waits for them, and re-layouts  4.16 us
    transpose x1, local copies, waits for them, and re-layouts, shards(): image = packed.reshape(bx // nshot, bys, nshot, zl).transpose(2, 0, 1, 3)  0.63 us

profile of v1, /device:TPU:0, one launch (start us, length us, event | category | flops | bytes accessed | tf_op | source)
XLA Modules:
  0.0 30.7 jit_solution(8415632523974350140)
XLA Ops:
  0.0 0.0 copy-start.7
  0.0 0.7 %copy-done.7 = s32[1,80,8]{1,2,0:T(8,128)S(1)} copy-done((s32[1,80,8]{1,2,0:T(8,128)S(1)}, s32[1,80,8]{1,2,0:T(8,128)}, u32[]{:S(2)}) %copy-start.7) | copy-done | bytes 2584
  0.7 0.0 copy-start.6
  0.7 0.1 copy.9
  0.8 0.6 %copy-done.6 = f32[1,4,80,8]{2,3,1,0:T(8,128)S(1)} copy-done((f32[1,4,80,8]{2,3,1,0:T(8,128)S(1)}, f32[1,4,80,8]{2,3,1,0:T(8,128)}, u32[]{:S(2)}) %copy-start.6) | copy-done | bytes 10264
  1.4 0.0 copy-start.2
  1.4 0.1 copy.10
  1.5 0.0 copy-start.3
  1.5 0.0 copy-start.4
  1.5 0.0 copy-start.5
  1.5 0.7 %copy-done.2 = f32[1,16,8,128]{3,2,1,0:T(8,128)S(1)} copy-done((f32[1,16,8,128]{3,2,1,0:T(8,128)S(1)}, f32[1,16,8,128]{3,2,1,0:T(8,128)}, u32[]{:S(2)}) %copy-start.2) | copy-done | bytes 65560
  2.2 0.0 copy-done.3
  2.2 0.0 copy-done.4
  2.3 0.0 copy-done.5
  2.3 0.0 copy-start
  2.3 1.0 %copy-done = bf16[1,2,80,8,128]{4,3,2,1,0:T(8,128)(2,1)S(1)} copy-done((bf16[1,2,80,8,128]{4,3,2,1,0:T(8,128)(2,1)S(1)}, bf16[1,2,80,8,128]{4,3,2,1,0:T(8,128)(2,1)}, u32[]{:S(2)}) %copy-start) | copy-done | bytes 327704
  3.2 0.0 copy-start.1
  3.2 1.0 %copy-done.1 = bf16[1,2,80,8,128]{4,3,2,1,0:T(8,128)(2,1)S(1)} copy-done((bf16[1,2,80,8,128]{4,3,2,1,0:T(8,128)(2,1)S(1)}, bf16[1,2,80,8,128]{4,3,2,1,0:T(8,128)(2,1)}, u32[]{:S(2)}) %copy-start.1) | copy-done | bytes 327704
  4.2 25.7 %shard_map.82 = f32[8,8,128]{2,1,0:T(8,128)S(1)} custom-call(f32[16,8,128]{2,1,0:T(8,128)S(1)} %bitcast.11, bf16[2,80,8,128]{3,2,1,0:T(8,128)(2,1)S(1)} %bitcast.8, bf16[2,80,8,128]{3,2,1,0:T(8,128)(2,1)S(1)} %bitcast.9, f32[1,4]{1,0:T(1,128)S(1)} %copy-done.3, s32[1,3]{1,0:T(1,128)S(1)} %copy-done.4, s32[1,2]{1,0:T(1,128)S(1)} %copy-done.5, ...), custom_call_target="tpu_custom_call" | custom-call | tf_op jit(solution)/shard_map/pallas_call | solution.py:288
  29.9 0.1 reshape.6
  30.0 0.6 %copy.11 = f32[2,8,8,64]{3,2,1,0:T(8,128)} copy(f32[2,8,8,64]{3,0,2,1:T(2,128)S(1)} %bitcast.12) | data formatting | bytes 65536 | tf_op jit(solution)/shard_map/transpose | solution.py:316
Async XLA Ops:
  0.0 0.7 %copy-start.7 = (s32[1,80,8]{1,2,0:T(8,128)S(1)}, s32[1,80,8]{1,2,0:T(8,128)}, u32[]{:S(2)}) copy-start(s32[1,80,8]{1,2,0:T(8,128)} %param.14) | copy-start | bytes 7684
  0.7 0.7 %copy-start.6 = (f32[1,4,80,8]{2,3,1,0:T(8,128)S(1)}, f32[1,4,80,8]{2,3,1,0:T(8,128)}, u32[]{:S(2)}) copy-start(f32[1,4,80,8]{2,3,1,0:T(8,128)} %param.15) | copy-start | bytes 30724
  1.4 0.8 %copy-start.2 = (f32[1,16,8,128]{3,2,1,0:T(8,128)S(1)}, f32[1,16,8,128]{3,2,1,0:T(8,128)}, u32[]{:S(2)}) copy-start(f32[1,16,8,128]{3,2,1,0:T(8,128)} %param.8) | copy-start | bytes 196612
  1.5 0.7 %copy-start.3 = (f32[1,4]{1,0:T(1,128)S(1)}, f32[1,4]{1,0:T(1,128)}, u32[]{:S(2)}) copy-start(f32[1,4]{1,0:T(1,128)} %wav.1) | copy-start | bytes 52
  1.5 0.7 %copy-start.4 = (s32[1,3]{1,0:T(1,128)S(1)}, s32[1,3]{1,0:T(1,128)}, u32[]{:S(2)}) copy-start(s32[1,3]{1,0:T(1,128)} %src.1) | copy-start | bytes 40
  1.5 0.7 %copy-start.5 = (s32[1,2]{1,0:T(1,128)S(1)}, s32[1,2]{1,0:T(1,128)}, u32[]{:S(2)}) copy-start(s32[1,2]{1,0:T(1,128)} %ap.1) | copy-start | bytes 28
  2.3 1.0 %copy-start = (bf16[1,2,80,8,128]{4,3,2,1,0:T(8,128)(2,1)S(1)}, bf16[1,2,80,8,128]{4,3,2,1,0:T(8,128)(2,1)}, u32[]{:S(2)}) copy-start(bf16[1,2,80,8,128]{4,3,2,1,0:T(8,128)(2,1)} %param.9) | copy-start | bytes 983044
  3.2 1.0 %copy-start.1 = (bf16[1,2,80,8,128]{4,3,2,1,0:T(8,128)(2,1)S(1)}, bf16[1,2,80,8,128]{4,3,2,1,0:T(8,128)(2,1)}, u32[]{:S(2)}) copy-start(bf16[1,2,80,8,128]{4,3,2,1,0:T(8,128)(2,1)} %param.10) | copy-start | bytes 983044

commit v2 on v1

v2 whole, which is shorter than its diff:
```python
import functools

import jax
import jax.numpy as jnp
from jax import lax
from jax.experimental import pallas as pl
from jax.experimental.pallas import tpu as pltpu
from jax.sharding import PartitionSpec as P

R = 2
STEPS = 4
NB = 2 * R + 1
MESH = pl.DeviceIdType.MESH

coeffs = (-205.0 / 72.0, 8.0 / 5.0, -1.0 / 5.0, 8.0 / 315.0, -1.0 / 560.0)
image_scale = 0.05
f32 = jnp.float32
bf16 = jnp.bfloat16


def kernel(nblock, nshot, vel, fwd, adj, wav, src, ap, mask, rec, out,
           F, A, W, ZF, ZA, PV, O, T, B, G, S, H, FI, AI, RI, MI,
           ls, vs, vr, fs, fr, as_, ar, gs, gr, ss, sr):
    bx, bys, bz = vel.shape
    home = lax.axis_index("block")
    team = lax.axis_index("shot")
    sub = lax.axis_index("sub")
    lo = jnp.maximum(R - home, 0)
    hi = jnp.minimum(R + nblock - home, NB)
    n = hi - lo
    offsets = [o for o in range(-R, R + 1) if o != 0]
    down = (2 * home < nblock).astype(jnp.int32)
    first = down * (hi - 1) + (1 - down) * lo
    turn = 1 - 2 * down

    def near(o):
        return (home + o >= 0) & (home + o < nblock)

    barrier = pltpu.get_barrier_semaphore()
    for o in offsets:
        @pl.when(near(o))
        def _():
            pl.semaphore_signal(barrier, inc=1, device_id={"block": home + o}, device_id_type=MESH)
    for r in range(1, nshot):
        pl.semaphore_signal(barrier, inc=1, device_id={"shot": lax.rem(team + r, nshot)}, device_id_type=MESH)
    pl.semaphore_signal(barrier, inc=1, device_id={"sub": 1 - sub}, device_id_type=MESH)

    local = [pltpu.make_async_copy(fwd, FI, ls.at[0]), pltpu.make_async_copy(adj, AI, ls.at[1]),
             pltpu.make_async_copy(rec, RI, ls.at[2]), pltpu.make_async_copy(mask, MI, ls.at[3]),
             pltpu.make_async_copy(vel, W.at[pl.ds(R * bx, bx)], ls.at[4])]
    for copy in local:
        copy.start()

    def keep_of(b):
        return jnp.where((b >= R - ap[0, 0]) & (b <= R + ap[0, 1]), 1.0, 0.0).astype(f32)

    def at(field, t, b):
        return field[t, pl.ds(4 + b * bx, bx), 8:16, :]

    def state(ref, t, b):
        rows = pl.ds(pl.multiple_of(t * NB * bx * bys + b * bx * bys, bx * bys), bx * bys)
        return ref[rows, :].astype(f32).reshape(bx, bys, bz)

    zx = jnp.zeros((4, 8, bz), f32)

    @pl.when(sub == 0)
    def _():
        lax.fori_loop(lo, hi, functools.partial(clear_at, F, A, 0, bx, bz), 0)

    @pl.when(sub == 1)
    def _():
        lax.fori_loop(lo, hi, functools.partial(clear_at, F, A, 16, bx, bz), 0)

    for field in (F, A):
        for t in range(STEPS):
            field[t, pl.ds(lo * bx, 4), 8:16, :] = zx
            field[t, pl.ds(4 + hi * bx, 4), 8:16, :] = zx

    pl.semaphore_wait(barrier, (n - 1) + (nshot - 1) + 1)

    def vel_copy(o):
        j = R - o
        return pltpu.make_async_remote_copy(
            src_ref=vel, dst_ref=W.at[pl.ds(j * bx, bx)], send_sem=vs.at[j], recv_sem=vr.at[j],
            device_id={"block": home + o}, device_id_type=MESH)

    for o in (-2, 2, -1, 1):
        @pl.when(near(o))
        def _():
            vel_copy(o).start()

    def rim(side, field, t, b, ssem, rsem):
        x = pl.ds(4 + b * bx, bx)
        return pltpu.make_async_remote_copy(
            src_ref=field.at[t, x, pl.ds(8 if side else 12, 4), :],
            dst_ref=field.at[t, x, pl.ds(16 if side else 4, 4), :],
            send_sem=ssem.at[t, b], recv_sem=rsem.at[t, b],
            device_id={"sub": 1 - sub}, device_id_type=MESH)

    def rim_start(t, b):
        for side in range(2):
            @pl.when(sub == side)
            def _():
                rim(side, F, t, b, fs, fr).start()
                rim(side, A, t, b, as_, ar).start()

    def rim_wait(t, b):
        for side in range(2):
            @pl.when(sub == side)
            def _():
                rim(1 - side, F, t, b, fs, fr).wait_recv()
                rim(1 - side, A, t, b, as_, ar).wait_recv()

    def rim_sent(t, b):
        for side in range(2):
            @pl.when(sub == side)
            def _():
                rim(side, F, t, b, fs, fr).wait_send()
                rim(side, A, t, b, as_, ar).wait_send()

    local[0].wait()
    local[1].wait()

    def load_states(i, c):
        b = first + turn * i
        kb = keep_of(b)
        rows = pl.ds(4 + b * bx, bx)
        F[0, rows, 8:16, :] = kb * state(FI, 1, b)
        A[0, rows, 8:16, :] = kb * state(AI, 1, b)
        rim_start(0, b)
        return c

    lax.fori_loop(0, n, load_states, 0)

    i0 = lax.broadcasted_iota(jnp.int32, (bz, bz), 0)
    i1 = lax.broadcasted_iota(jnp.int32, (bz, bz), 1)
    dist = jnp.abs(i0 - i1)
    band = jnp.where(dist == 0, 3.0 * coeffs[0], 0.0).astype(f32)
    for j in range(1, 5):
        band = jnp.where(dist == j, coeffs[j], band)
    band_hi = band.astype(bf16)
    band_lo = (band - band_hi.astype(f32)).astype(bf16)
    B[0:bz, 0:bz] = band_hi
    B[bz:2 * bz, 0:bz] = band_hi
    B[0:bz, bz:2 * bz] = band_lo
    B[bz:2 * bz, bz:2 * bz] = jnp.zeros((bz, bz), bf16)

    ox = lax.broadcasted_iota(jnp.int32, (bx, bys, bz), 0)
    oy = lax.broadcasted_iota(jnp.int32, (bx, bys, bz), 1) + sub * bys
    oz = lax.broadcasted_iota(jnp.int32, (bx, bys, bz), 2)
    O[...] = jnp.where((ox == src[0, 0]) & (oy == src[0, 1]) & (oz == src[0, 2]), 1.0, 0.0).astype(f32)
    local[2].wait()
    local[3].wait()
    local[4].wait()
    live = MI[...].astype(f32)
    T[...] = jnp.zeros_like(T)
    for t in range(STEPS):
        T[t, :, 0:NB * bx] = live * RI[t]
    surface = lax.broadcasted_iota(jnp.int32, (bys, bz), 1) == 0

    def laplace(t, b):
        flat = jnp.concatenate([at(F, t, b).reshape(bx * bys, bz), at(A, t, b).reshape(bx * bys, bz)], axis=0)
        high = flat.astype(bf16)
        low = (flat - high.astype(f32)).astype(bf16)
        both = jnp.concatenate([high, low], axis=1)
        prod = jnp.dot(both, B[...], preferred_element_type=f32)
        depth = prod[:, :bz] + prod[:, bz:]
        result = []
        for k, field in enumerate((F, A)):
            total = depth[k * bx * bys:(k + 1) * bx * bys].reshape(bx, bys, bz)
            for j in range(1, 5):
                total = total + coeffs[j] * (
                    field[t, pl.ds(4 + j + b * bx, bx), 8:16, :] + field[t, pl.ds(4 - j + b * bx, bx), 8:16, :]
                    + field[t, pl.ds(4 + b * bx, bx), 8 + j:16 + j, :] + field[t, pl.ds(4 + b * bx, bx), 8 - j:16 - j, :])
            result.append(total)
        return result

    def source_term(step, b):
        return jnp.where(b == R, wav[0, step], 0.0) * O[...]

    def receiver_term(step, b):
        row = pltpu.roll(T[STEPS - 1 - step], 128 - b * bx, 1) * keep_of(b)
        parts = []
        for x in range(bx):
            moved = pltpu.roll(row, 128 - x, 1) if x else row
            parts.append(jnp.where(surface, moved, 0.0)[None])
        return jnp.concatenate(parts, axis=0)

    def first_diff(i, c):
        b = first + turn * i
        rim_wait(0, b)
        cells = pl.ds(b * bx, bx)
        ZF[cells], ZA[cells] = laplace(0, b)
        return c

    lax.fori_loop(0, n, first_diff, 0)

    def image_copy(j):
        return pltpu.make_async_remote_copy(
            src_ref=PV.at[pl.ds(j * bx, bx)], dst_ref=G.at[j], send_sem=gs.at[j], recv_sem=gr.at[j],
            device_id={"block": home + j - R}, device_id_type=MESH)

    def vel_wait(b):
        pltpu.make_async_remote_copy(
            src_ref=vel, dst_ref=W.at[pl.ds(b * bx, bx)], send_sem=vs.at[b], recv_sem=vr.at[b],
            device_id={"block": home + b - R}, device_id_type=MESH).wait_recv()

    def advance(step, b):
        last = step == STEPS - 1
        cells = pl.ds(b * bx, bx)
        if step == 0:
            @pl.when(b != R)
            def _():
                vel_wait(b)
            kb = keep_of(b)
            w = kb * W[cells]
            W[cells] = w
            lap_f, lap_a = ZF[cells], ZA[cells]
            old_f, old_a = kb * state(FI, 0, b), kb * state(AI, 0, b)
        else:
            rim_wait(step, b)
            w = W[cells]
            lap_f, lap_a = laplace(step, b)
            old_f, old_a = at(F, step - 1, b), at(A, step - 1, b)
        new_f = 2.0 * at(F, step, b) - old_f + w * lap_f + source_term(step, b)
        new_a = 2.0 * at(A, step, b) - old_a + w * lap_a + receiver_term(step, b)
        if not last:
            F[step + 1, pl.ds(4 + b * bx, bx), 8:16, :] = new_f
            A[step + 1, pl.ds(4 + b * bx, bx), 8:16, :] = new_a
            rim_start(step + 1, b)
        if step == 1:
            PV[cells] = new_f * new_a
        elif step > 1:
            early = STEPS - 1 - step
            PV[cells] = PV[cells] + new_f * at(A, early, b) + at(F, early, b) * new_a
        if last:
            @pl.when(b != R)
            def _():
                image_copy(b).start()

    def wave(k, c):
        for step in range(STEPS):
            @pl.when((k >= step) & (k - step < n))
            def _():
                advance(step, first + turn * (k - step))
        return c

    lax.fori_loop(0, n + STEPS - 1, wave, 0)

    H[...] = PV[R * bx:(R + 1) * bx]
    for o in (-1, 1, -2, 2):
        @pl.when(near(o))
        def _():
            j = R - o
            image_copy(j).wait_recv()
            H[...] = H[...] + G[j]

    zl = bz // nshot
    xg = bx // nshot
    lane = lax.broadcasted_iota(jnp.int32, (xg, bys, bz), 2)

    def packed(d):
        total = jnp.zeros((xg, bys, bz), f32)
        for k in range(nshot):
            shift = lax.rem((k - d + nshot) * zl, bz)
            moved = pltpu.roll(H[k * xg:(k + 1) * xg].reshape(xg * bys, bz), shift, 1).reshape(xg, bys, bz)
            total = jnp.where((lane >= k * zl) & (lane < (k + 1) * zl), moved, total)
        return total

    def team_copy(r):
        return pltpu.make_async_remote_copy(
            src_ref=S.at[r], dst_ref=S.at[nshot + r], send_sem=ss.at[r], recv_sem=sr.at[r],
            device_id={"shot": lax.rem(team + r, nshot)}, device_id_type=MESH)

    for r in range(1, nshot):
        S[r] = packed(lax.rem(team + r, nshot))
        team_copy(r).start()
    total = packed(team)
    for r in range(1, nshot):
        team_copy(r).wait_recv()
        total = total + S[nshot + r]
    out[...] = image_scale * total

    def sent(b, c):
        for t in range(STEPS):
            rim_sent(t, b)
        return c

    lax.fori_loop(lo, hi, sent, 0)
    for o in offsets:
        @pl.when(near(o))
        def _():
            vel_copy(o).wait_send()
            image_copy(R + o).wait_send()
    for r in range(1, nshot):
        team_copy(r).wait_send()


def clear_at(F, A, row, bx, bz, b, c):
    for field in (F, A):
        for t in range(STEPS):
            field[t, pl.ds(4 + b * bx, bx), row:row + 8, :] = jnp.zeros((bx, 8, bz), f32)
    return c


def shards(nblock, nshot, vel_sq, fwd_state, adj_state, wavelet, source, aperture, rec_mask, rec_data):
    bx, bys, bz = vel_sq.shape[1:]
    width = NB * bx
    vmem = pl.BlockSpec(memory_space=pltpu.VMEM)
    hbm = pl.BlockSpec(memory_space=pltpu.HBM)
    smem = pl.BlockSpec(memory_space=pltpu.SMEM)
    dma = pltpu.SemaphoreType.DMA
    packed = pl.pallas_call(
        functools.partial(kernel, nblock, nshot),
        out_shape=jax.ShapeDtypeStruct((bx // nshot, bys, bz), f32),
        in_specs=[hbm, hbm, hbm, smem, smem, smem, hbm, hbm],
        out_specs=vmem,
        scratch_shapes=[
            pltpu.VMEM((STEPS, width + 8, 24, bz), f32),
            pltpu.VMEM((STEPS, width + 8, 24, bz), f32),
            pltpu.VMEM((width, bys, bz), f32),
            pltpu.VMEM((width, bys, bz), f32),
            pltpu.VMEM((width, bys, bz), f32),
            pltpu.VMEM((width, bys, bz), f32),
            pltpu.VMEM((bx, bys, bz), f32),
            pltpu.VMEM((STEPS, bys, bz), f32),
            pltpu.VMEM((2 * bz, 2 * bz), bf16),
            pltpu.VMEM((NB, bx, bys, bz), f32),
            pltpu.VMEM((2 * nshot, bx // nshot, bys, bz), f32),
            pltpu.VMEM((bx, bys, bz), f32),
            pltpu.VMEM((2 * width * bys, bz), bf16),
            pltpu.VMEM((2 * width * bys, bz), bf16),
            pltpu.VMEM((STEPS, bys, width), f32),
            pltpu.VMEM((bys, width), jnp.int32),
            dma((5,)),
            dma((NB,)), dma((NB,)),
            dma((STEPS, NB)), dma((STEPS, NB)),
            dma((STEPS, NB)), dma((STEPS, NB)),
            dma((NB,)), dma((NB,)),
            dma((nshot,)), dma((nshot,)),
        ],
        compiler_params=pltpu.CompilerParams(
            collective_id=0, has_side_effects=True, vmem_limit_bytes=63 * 1024 * 1024),
    )(vel_sq[0], fwd_state.reshape(-1, bz), adj_state.reshape(-1, bz), wavelet, source, aperture,
      rec_mask[0].T, rec_data[0].transpose(0, 2, 1))
    zl = bz // nshot
    image = packed.reshape(bx // nshot, bys, nshot, zl).transpose(2, 0, 1, 3)
    return image.reshape(1, bx, bys, zl)


def solution(mesh):
    placed = (
        P(("parts", "block"), None, "sub", None),
        P(("parts", "block", "shot"), None, None, "sub", None),
        P(("parts", "block", "shot"), None, None, "sub", None),
        P(("parts", "block", "shot"), None),
        P(("parts", "block", "shot"), None),
        P(("parts", "block", "shot"), None),
        P(("parts", "block", "shot"), None, "sub"),
        P(("parts", "block", "shot"), None, None, "sub"),
    )
    return jax.shard_map(
        functools.partial(shards, mesh.shape["block"], mesh.shape["shot"]),
        mesh=mesh,
        in_specs=placed,
        out_specs=P(("parts", "block"), None, "sub", "shot"),
        check_vma=False,
    )
```

time: 31 us -> 26.9 us (0.87)
  local copies, waits for them, and re-layouts: 4.89 us -> 1.49 us
  Pallas kernels: 25.7 us -> 25.2 us
    unnamed x18 -> x0, local copies, waits for them, and re-layouts: 4.16 us -> none
    reshape x1, local copies, waits for them, and re-layouts: 0.1 us -> 0.85 us  [shards(): image = packed.reshape(bx // nshot, bys, nshot, zl).transpose(2, 0, 1, 3)]
    pallas_call x1, Pallas kernels: 25.7 us -> 25.2 us  [shards(): pl.pallas_call(functools.partial(kernel, nblock, nshot), out_shape=jax.Sh...]
where the time goes in v2:
time: 26.9 us; the launch traced here: 26.7 us
  Pallas kernels  25.2 us (94%)
  local copies, waits for them, and re-layouts  1.49 us (6%)
    pallas_call x1, Pallas kernels, shards(): pl.pallas_call(functools.partial(kernel, nblock, nshot), out_shape=jax.Sh...  25.2 us
    reshape x1, local copies, waits for them, and re-layouts, shards(): image = packed.reshape(bx // nshot, bys, nshot, zl).transpose(2, 0, 1, 3)  0.85 us
    transpose x1, local copies, waits for them, and re-layouts, shards(): image = packed.reshape(bx // nshot, bys, nshot, zl).transpose(2, 0, 1, 3)  0.63 us

profile of v2, /device:TPU:0, one launch (start us, length us, event | category | flops | bytes accessed | tf_op | source)
XLA Modules:
  0.0 26.7 jit_solution(15496448272279631382)
XLA Ops:
  0.0 25.2 %shard_map.82 = f32[8,8,128]{2,1,0:T(8,128)} custom-call(f32[16,8,128]{2,1,0:T(8,128)} %bitcast.14, bf16[1280,128]{1,0:T(8,128)(2,1)} %bitcast.11, bf16[1280,128]{1,0:T(8,128)(2,1)} %bitcast.12, f32[1,4]{1,0:T(1,128)} %wav.1, s32[1,3]{1,0:T(1,128)} %src.1, s32[1,2]{1,0:T(1,128)} %ap.1, s32[8,80]{1,0:T(8,128)} %bitcast.16, f32[4,8,80]{2,1,0:T(8,128)} %bitcast.15), custom_call_target="tpu_custom_call" | custom-call | tf_op jit(solution)/shard_map/pallas_call | solution.py:313
  25.2 0.9 %reshape.14 = f32[8,8,2,64]{3,2,1,0:T(2,128)S(1)} reshape(f32[8,8,128]{2,1,0:T(8,128)} %shard_map.82) | data formatting | bytes 65536 | tf_op jit(solution)/shard_map/reshape | solution.py:347
  26.1 0.6 %copy.9 = f32[2,8,8,64]{3,2,1,0:T(8,128)} copy(f32[2,8,8,64]{3,0,2,1:T(2,128)S(1)} %bitcast.13) | data formatting | bytes 65536 | tf_op jit(solution)/shard_map/transpose | solution.py:347

commit v3 on v2

--- a/solution.py
+++ b/solution.py
@@ -14,12 +14,14 @@
 
 coeffs = (-205.0 / 72.0, 8.0 / 5.0, -1.0 / 5.0, 8.0 / 315.0, -1.0 / 560.0)
 image_scale = 0.05
+vel_mid = 0.12
+vel_step = 0.06 / 32000.0
 f32 = jnp.float32
 bf16 = jnp.bfloat16
 
 
 def kernel(nblock, nshot, vel, fwd, adj, wav, src, ap, mask, rec, out,
-           F, A, W, ZF, ZA, PV, O, T, B, G, S, H, FI, AI, RI, MI,
+           F, A, W, ZF, ZA, PV, O, T, B, G, S, H, FI, AI, RI, MI, VC, VG,
            ls, vs, vr, fs, fr, as_, ar, gs, gr, ss, sr):
     bx, bys, bz = vel.shape
     home = lax.axis_index("block")
@@ -48,7 +50,7 @@
     local = [pltpu.make_async_copy(fwd, FI, ls.at[0]), pltpu.make_async_copy(adj, AI, ls.at[1]),
              pltpu.make_async_copy(rec, RI, ls.at[2]), pltpu.make_async_copy(mask, MI, ls.at[3]),
              pltpu.make_async_copy(vel, W.at[pl.ds(R * bx, bx)], ls.at[4])]
-    for copy in local:
+    for copy in local[::-1]:
         copy.start()
 
     def keep_of(b):
@@ -76,12 +78,16 @@
             field[t, pl.ds(lo * bx, 4), 8:16, :] = zx
             field[t, pl.ds(4 + hi * bx, 4), 8:16, :] = zx
 
+    local[4].wait()
+    code = jnp.round((W[R * bx:(R + 1) * bx].reshape(bx * bys, bz) - vel_mid) * (1.0 / vel_step))
+    VC[...] = code.astype(jnp.int32).astype(jnp.int16)
+
     pl.semaphore_wait(barrier, (n - 1) + (nshot - 1) + 1)
 
     def vel_copy(o):
         j = R - o
         return pltpu.make_async_remote_copy(
-            src_ref=vel, dst_ref=W.at[pl.ds(j * bx, bx)], send_sem=vs.at[j], recv_sem=vr.at[j],
+            src_ref=VC, dst_ref=VG.at[j], send_sem=vs.at[j], recv_sem=vr.at[j],
             device_id={"block": home + o}, device_id_type=MESH)
 
     for o in (-2, 2, -1, 1):
@@ -151,7 +157,6 @@
     O[...] = jnp.where((ox == src[0, 0]) & (oy == src[0, 1]) & (oz == src[0, 2]), 1.0, 0.0).astype(f32)
     local[2].wait()
     local[3].wait()
-    local[4].wait()
     live = MI[...].astype(f32)
     T[...] = jnp.zeros_like(T)
     for t in range(STEPS):
@@ -202,7 +207,7 @@
 
     def vel_wait(b):
         pltpu.make_async_remote_copy(
-            src_ref=vel, dst_ref=W.at[pl.ds(b * bx, bx)], send_sem=vs.at[b], recv_sem=vr.at[b],
+            src_ref=VC, dst_ref=VG.at[b], send_sem=vs.at[b], recv_sem=vr.at[b],
             device_id={"block": home + b - R}, device_id_type=MESH).wait_recv()
 
     def advance(step, b):
@@ -212,6 +217,7 @@
             @pl.when(b != R)
             def _():
                 vel_wait(b)
+                W[cells] = (VG[b].astype(jnp.int32).astype(f32) * vel_step + vel_mid).reshape(bx, bys, bz)
             kb = keep_of(b)
             w = kb * W[cells]
             W[cells] = w
@@ -279,7 +285,11 @@
     for r in range(1, nshot):
         team_copy(r).wait_recv()
         total = total + S[nshot + r]
-    out[...] = image_scale * total
+    total = image_scale * total
+    for k in range(nshot):
+        flat = total.reshape(xg * bys, bz)
+        moved = pltpu.roll(flat, bz - k * zl, 1) if k else flat
+        out[k * xg:(k + 1) * xg] = moved.reshape(xg, bys, bz)[:, :, :zl]
 
     def sent(b, c):
         for t in range(STEPS):
@@ -310,9 +320,9 @@
     hbm = pl.BlockSpec(memory_space=pltpu.HBM)
     smem = pl.BlockSpec(memory_space=pltpu.SMEM)
     dma = pltpu.SemaphoreType.DMA
-    packed = pl.pallas_call(
+    image = pl.pallas_call(
         functools.partial(kernel, nblock, nshot),
-        out_shape=jax.ShapeDtypeStruct((bx // nshot, bys, bz), f32),
+        out_shape=jax.ShapeDtypeStruct((bx, bys, bz // nshot), f32),
         in_specs=[hbm, hbm, hbm, smem, smem, smem, hbm, hbm],
         out_specs=vmem,
         scratch_shapes=[
@@ -332,6 +342,8 @@
             pltpu.VMEM((2 * width * bys, bz), bf16),
             pltpu.VMEM((STEPS, bys, width), f32),
             pltpu.VMEM((bys, width), jnp.int32),
+            pltpu.VMEM((bx * bys, bz), jnp.int16),
+            pltpu.VMEM((NB, bx * bys, bz), jnp.int16),
             dma((5,)),
             dma((NB,)), dma((NB,)),
             dma((STEPS, NB)), dma((STEPS, NB)),
@@ -343,9 +355,7 @@
             collective_id=0, has_side_effects=True, vmem_limit_bytes=63 * 1024 * 1024),
     )(vel_sq[0], fwd_state.reshape(-1, bz), adj_state.reshape(-1, bz), wavelet, source, aperture,
       rec_mask[0].T, rec_data[0].transpose(0, 2, 1))
-    zl = bz // nshot
-    image = packed.reshape(bx // nshot, bys, nshot, zl).transpose(2, 0, 1, 3)
-    return image.reshape(1, bx, bys, zl)
+    return image[None]
 
 
 def solution(mesh):

time: 26.9 us -> 25.4 us (0.944)
  Pallas kernels: 25.2 us -> 23.7 us
    pallas_call x1, Pallas kernels: 25.2 us -> 23.7 us  [shards(): pl.pallas_call(functools.partial(kernel, nblock, nshot), out_shape=jax.Sh...]
    unnamed x0 -> x1, local copies, waits for them, and re-layouts: none -> 1.47 us
    reshape x1 -> x0, local copies, waits for them, and re-layouts: 0.85 us -> none  [shards(): image = packed.reshape(bx // nshot, bys, nshot, zl).transpose(2, 0, 1, 3)]
    transpose x1 -> x0, local copies, waits for them, and re-layouts: 0.63 us -> none  [shards(): image = packed.reshape(bx // nshot, bys, nshot, zl).transpose(2, 0, 1, 3)]
where the time goes in v3:
time: 25.4 us; the launch traced here: 25.2 us
  Pallas kernels  23.7 us (93%)
  local copies, waits for them, and re-layouts  1.47 us (6%)
    pallas_call x1, Pallas kernels, shards(): pl.pallas_call(functools.partial(kernel, nblock, nshot), out_shape=jax.Sh...  23.7 us
    unnamed x1, local copies, waits for them, and re-layouts  1.47 us

profile of v3, /device:TPU:0, one launch (start us, length us, event | category | flops | bytes accessed | tf_op | source)
XLA Modules:
  0.0 25.2 jit_solution(71387314022538599)
XLA Ops:
  0.0 23.7 %shard_map.82 = f32[16,8,64]{2,1,0:T(8,128)} custom-call(f32[16,8,128]{2,1,0:T(8,128)} %bitcast.13, bf16[1280,128]{1,0:T(8,128)(2,1)} %bitcast.10, bf16[1280,128]{1,0:T(8,128)(2,1)} %bitcast.11, f32[1,4]{1,0:T(1,128)} %wav.1, s32[1,3]{1,0:T(1,128)} %src.1, s32[1,2]{1,0:T(1,128)} %ap.1, s32[8,80]{1,0:T(8,128)} %bitcast.15, f32[4,8,80]{2,1,0:T(8,128)} %bitcast.14), custom_call_target="tpu_custom_call" | custom-call | tf_op jit(solution)/shard_map/pallas_call | solution.py:323
  23.7 1.5 %copy.10 = f32[1,16,8,64]{3,2,1,0:T(8,128)} copy(f32[1,16,8,64]{3,2,1,0:T(8,128)} %bitcast.12) | data formatting | bytes 65536

commit v4 on v3

--- a/solution.py
+++ b/solution.py
@@ -21,7 +21,7 @@
 
 
 def kernel(nblock, nshot, vel, fwd, adj, wav, src, ap, mask, rec, out,
-           F, A, W, ZF, ZA, PV, O, T, B, G, S, H, FI, AI, RI, MI, VC, VG,
+           F, A, W, ZF, ZA, PV, O, T, B, G, SP, SR, M, FI, AI, RI, MI, VC, VG,
            ls, vs, vr, fs, fr, as_, ar, gs, gr, ss, sr):
     bx, bys, bz = vel.shape
     home = lax.axis_index("block")
@@ -202,8 +202,37 @@
 
     def image_copy(j):
         return pltpu.make_async_remote_copy(
-            src_ref=PV.at[pl.ds(j * bx, bx)], dst_ref=G.at[j], send_sem=gs.at[j], recv_sem=gr.at[j],
+            src_ref=M.at[j], dst_ref=G.at[j], send_sem=gs.at[j], recv_sem=gr.at[j],
             device_id={"block": home + j - R}, device_id_type=MESH)
+
+    zl = bz // nshot
+    xg = bx // nshot
+    lane = lax.broadcasted_iota(jnp.int32, (xg, bys, bz), 2)
+
+    def packed(b, d):
+        total = jnp.zeros((xg, bys, bz), f32)
+        for k in range(nshot):
+            shift = lax.rem((k - d + nshot) * zl, bz)
+            layers = PV[pl.ds(b * bx + k * xg, xg)].reshape(xg * bys, bz)
+            moved = pltpu.roll(layers, shift, 1).reshape(xg, bys, bz)
+            total = jnp.where((lane >= k * zl) & (lane < (k + 1) * zl), moved, total)
+        return total
+
+    def team_copy(b, r):
+        return pltpu.make_async_remote_copy(
+            src_ref=SP.at[b, r], dst_ref=SR.at[b, r], send_sem=ss.at[b, r], recv_sem=sr.at[b, r],
+            device_id={"shot": lax.rem(team + r, nshot)}, device_id_type=MESH)
+
+    def finish(b):
+        total = M[b]
+        for r in range(1, nshot):
+            team_copy(b, r).wait_recv()
+            total = total + SR[b, r]
+        M[b] = total
+
+        @pl.when(b != R)
+        def _():
+            image_copy(b).start()
 
     def vel_wait(b):
         pltpu.make_async_remote_copy(
@@ -240,51 +269,32 @@
             early = STEPS - 1 - step
             PV[cells] = PV[cells] + new_f * at(A, early, b) + at(F, early, b) * new_a
         if last:
-            @pl.when(b != R)
-            def _():
-                image_copy(b).start()
+            for r in range(1, nshot):
+                SP[b, r] = packed(b, lax.rem(team + r, nshot))
+                team_copy(b, r).start()
+            M[b] = packed(b, team)
 
     def wave(k, c):
         for step in range(STEPS):
             @pl.when((k >= step) & (k - step < n))
             def _():
                 advance(step, first + turn * (k - step))
+
+        @pl.when(k >= STEPS)
+        def _():
+            finish(first + turn * (k - STEPS))
         return c
 
-    lax.fori_loop(0, n + STEPS - 1, wave, 0)
-
-    H[...] = PV[R * bx:(R + 1) * bx]
+    lax.fori_loop(0, n + STEPS, wave, 0)
+
     for o in (-1, 1, -2, 2):
         @pl.when(near(o))
         def _():
             j = R - o
             image_copy(j).wait_recv()
-            H[...] = H[...] + G[j]
-
-    zl = bz // nshot
-    xg = bx // nshot
-    lane = lax.broadcasted_iota(jnp.int32, (xg, bys, bz), 2)
-
-    def packed(d):
-        total = jnp.zeros((xg, bys, bz), f32)
-        for k in range(nshot):
-            shift = lax.rem((k - d + nshot) * zl, bz)
-            moved = pltpu.roll(H[k * xg:(k + 1) * xg].reshape(xg * bys, bz), shift, 1).reshape(xg, bys, bz)
-            total = jnp.where((lane >= k * zl) & (lane < (k + 1) * zl), moved, total)
-        return total
-
-    def team_copy(r):
-        return pltpu.make_async_remote_copy(
-            src_ref=S.at[r], dst_ref=S.at[nshot + r], send_sem=ss.at[r], recv_sem=sr.at[r],
-            device_id={"shot": lax.rem(team + r, nshot)}, device_id_type=MESH)
-
-    for r in range(1, nshot):
-        S[r] = packed(lax.rem(team + r, nshot))
-        team_copy(r).start()
-    total = packed(team)
-    for r in range(1, nshot):
-        team_copy(r).wait_recv()
-        total = total + S[nshot + r]
+            M[R] = M[R] + G[j]
+
+    total = M[R]
     total = image_scale * total
     for k in range(nshot):
         flat = total.reshape(xg * bys, bz)
@@ -294,6 +304,8 @@
     def sent(b, c):
         for t in range(STEPS):
             rim_sent(t, b)
+        for r in range(1, nshot):
+            team_copy(b, r).wait_send()
         return c
 
     lax.fori_loop(lo, hi, sent, 0)
@@ -302,8 +314,6 @@
         def _():
             vel_copy(o).wait_send()
             image_copy(R + o).wait_send()
-    for r in range(1, nshot):
-        team_copy(r).wait_send()
 
 
 def clear_at(F, A, row, bx, bz, b, c):
@@ -335,9 +345,10 @@
             pltpu.VMEM((bx, bys, bz), f32),
             pltpu.VMEM((STEPS, bys, bz), f32),
             pltpu.VMEM((2 * bz, 2 * bz), bf16),
-            pltpu.VMEM((NB, bx, bys, bz), f32),
-            pltpu.VMEM((2 * nshot, bx // nshot, bys, bz), f32),
-            pltpu.VMEM((bx, bys, bz), f32),
+            pltpu.VMEM((NB, bx // nshot, bys, bz), f32),
+            pltpu.VMEM((NB, nshot, bx // nshot, bys, bz), f32),
+            pltpu.VMEM((NB, nshot, bx // nshot, bys, bz), f32),
+            pltpu.VMEM((NB, bx // nshot, bys, bz), f32),
             pltpu.VMEM((2 * width * bys, bz), bf16),
             pltpu.VMEM((2 * width * bys, bz), bf16),
             pltpu.VMEM((STEPS, bys, width), f32),
@@ -349,7 +360,7 @@
             dma((STEPS, NB)), dma((STEPS, NB)),
             dma((STEPS, NB)), dma((STEPS, NB)),
             dma((NB,)), dma((NB,)),
-            dma((nshot,)), dma((nshot,)),
+            dma((NB, nshot)), dma((NB, nshot)),
         ],
         compiler_params=pltpu.CompilerParams(
             collective_id=0, has_side_effects=True, vmem_limit_bytes=63 * 1024 * 1024),

time: 25.4 us -> 26.4 us (1.039)
  Pallas kernels: 23.7 us -> 24.7 us
    pallas_call x1, Pallas kernels: 23.7 us -> 24.7 us  [shards(): pl.pallas_call(functools.partial(kernel, nblock, nshot), out_shape=jax.Sh...]
where the time goes in v4:
time: 26.4 us; the launch traced here: 26.2 us
  Pallas kernels  24.7 us (94%)
  local copies, waits for them, and re-layouts  1.47 us (6%)
    pallas_call x1, Pallas kernels, shards(): pl.pallas_call(functools.partial(kernel, nblock, nshot), out_shape=jax.Sh...  24.7 us
    unnamed x1, local copies, waits for them, and re-layouts  1.47 us

profile of v4, /device:TPU:0, one launch (start us, length us, event | category | flops | bytes accessed | tf_op | source)
XLA Modules:
  0.0 26.2 jit_solution(10334063962515973025)
XLA Ops:
  0.0 24.7 %shard_map.82 = f32[16,8,64]{2,1,0:T(8,128)} custom-call(f32[16,8,128]{2,1,0:T(8,128)} %bitcast.13, bf16[1280,128]{1,0:T(8,128)(2,1)} %bitcast.10, bf16[1280,128]{1,0:T(8,128)(2,1)} %bitcast.11, f32[1,4]{1,0:T(1,128)} %wav.1, s32[1,3]{1,0:T(1,128)} %src.1, s32[1,2]{1,0:T(1,128)} %ap.1, s32[8,80]{1,0:T(8,128)} %bitcast.15, f32[4,8,80]{2,1,0:T(8,128)} %bitcast.14), custom_call_target="tpu_custom_call" | custom-call | tf_op jit(solution)/shard_map/pallas_call | solution.py:333
  24.8 1.5 %copy.10 = f32[1,16,8,64]{3,2,1,0:T(8,128)} copy(f32[1,16,8,64]{3,2,1,0:T(8,128)} %bitcast.12) | data formatting | bytes 65536

commit v5 on v3

--- a/solution.py
+++ b/solution.py
@@ -21,9 +21,10 @@
 
 
 def kernel(nblock, nshot, vel, fwd, adj, wav, src, ap, mask, rec, out,
-           F, A, W, ZF, ZA, PV, O, T, B, G, S, H, FI, AI, RI, MI, VC, VG,
-           ls, vs, vr, fs, fr, as_, ar, gs, gr, ss, sr):
+           FA, W, ZF, ZA, PV, O, T, B, G, S, H, FI, AI, RI, MI, VC, VG,
+           ls, vs, vr, fs, fr, gs, gr, ss, sr):
     bx, bys, bz = vel.shape
+    F, A = FA.at[:, 0], FA.at[:, 1]
     home = lax.axis_index("block")
     team = lax.axis_index("shot")
     sub = lax.axis_index("sub")
@@ -95,34 +96,31 @@
         def _():
             vel_copy(o).start()
 
-    def rim(side, field, t, b, ssem, rsem):
+    def rim(side, t, b):
         x = pl.ds(4 + b * bx, bx)
         return pltpu.make_async_remote_copy(
-            src_ref=field.at[t, x, pl.ds(8 if side else 12, 4), :],
-            dst_ref=field.at[t, x, pl.ds(16 if side else 4, 4), :],
-            send_sem=ssem.at[t, b], recv_sem=rsem.at[t, b],
+            src_ref=FA.at[t, :, x, pl.ds(8 if side else 12, 4), :],
+            dst_ref=FA.at[t, :, x, pl.ds(16 if side else 4, 4), :],
+            send_sem=fs.at[t, b], recv_sem=fr.at[t, b],
             device_id={"sub": 1 - sub}, device_id_type=MESH)
 
     def rim_start(t, b):
         for side in range(2):
             @pl.when(sub == side)
             def _():
-                rim(side, F, t, b, fs, fr).start()
-                rim(side, A, t, b, as_, ar).start()
+                rim(side, t, b).start()
 
     def rim_wait(t, b):
         for side in range(2):
             @pl.when(sub == side)
             def _():
-                rim(1 - side, F, t, b, fs, fr).wait_recv()
-                rim(1 - side, A, t, b, as_, ar).wait_recv()
+                rim(1 - side, t, b).wait_recv()
 
     def rim_sent(t, b):
         for side in range(2):
             @pl.when(sub == side)
             def _():
-                rim(side, F, t, b, fs, fr).wait_send()
-                rim(side, A, t, b, as_, ar).wait_send()
+                rim(side, t, b).wait_send()
 
     local[0].wait()
     local[1].wait()
@@ -326,8 +324,7 @@
         in_specs=[hbm, hbm, hbm, smem, smem, smem, hbm, hbm],
         out_specs=vmem,
         scratch_shapes=[
-            pltpu.VMEM((STEPS, width + 8, 24, bz), f32),
-            pltpu.VMEM((STEPS, width + 8, 24, bz), f32),
+            pltpu.VMEM((STEPS, 2, width + 8, 24, bz), f32),
             pltpu.VMEM((width, bys, bz), f32),
             pltpu.VMEM((width, bys, bz), f32),
             pltpu.VMEM((width, bys, bz), f32),
@@ -347,7 +344,6 @@
             dma((5,)),
             dma((NB,)), dma((NB,)),
             dma((STEPS, NB)), dma((STEPS, NB)),
-            dma((STEPS, NB)), dma((STEPS, NB)),
             dma((NB,)), dma((NB,)),
             dma((nshot,)), dma((nshot,)),
         ],

time: 25.4 us -> 25 us (0.984)
  Pallas kernels: 23.7 us -> 23.3 us
    pallas_call x1, Pallas kernels: 23.7 us -> 23.3 us  [shards(): pl.pallas_call(functools.partial(kernel, nblock, nshot), out_shape=jax.Sh...]
where the time goes in v5:
time: 25 us; the launch traced here: 24.8 us
  Pallas kernels  23.3 us (93%)
  local copies, waits for them, and re-layouts  1.47 us (6%)
    pallas_call x1, Pallas kernels, shards(): pl.pallas_call(functools.partial(kernel, nblock, nshot), out_shape=jax.Sh...  23.3 us
    unnamed x1, local copies, waits for them, and re-layouts  1.47 us

profile of v5, /device:TPU:0, one launch (start us, length us, event | category | flops | bytes accessed | tf_op | source)
XLA Modules:
  0.0 24.8 jit_solution(11488725285050588378)
XLA Ops:
  0.0 23.3 %shard_map.82 = f32[16,8,64]{2,1,0:T(8,128)} custom-call(f32[16,8,128]{2,1,0:T(8,128)} %bitcast.13, bf16[1280,128]{1,0:T(8,128)(2,1)} %bitcast.10, bf16[1280,128]{1,0:T(8,128)(2,1)} %bitcast.11, f32[1,4]{1,0:T(1,128)} %wav.1, s32[1,3]{1,0:T(1,128)} %src.1, s32[1,2]{1,0:T(1,128)} %ap.1, s32[8,80]{1,0:T(8,128)} %bitcast.15, f32[4,8,80]{2,1,0:T(8,128)} %bitcast.14), custom_call_target="tpu_custom_call" | custom-call | tf_op jit(solution)/shard_map/pallas_call | solution.py:321
  23.3 1.5 %copy.10 = f32[1,16,8,64]{3,2,1,0:T(8,128)} copy(f32[1,16,8,64]{3,2,1,0:T(8,128)} %bitcast.12) | data formatting | bytes 65536
